TPU v7x, 128 devices: a whole 4x4x4 slice. The times are simulated.
128 devices in a mesh: dp: 8 (over x, core), tensor: 16 (over z, y).
Axes of the slice: x: 4, y: 4, z: 4, core: 2. Of those that a mesh axis runs over, the one named last changes fastest.
Arguments:
- tokens: bfloat16 [16384, 8192], P(('dp', 'tensor')), parts along dimension 0, may hold values from -6 to 6
- route_order: int32 [128, 128], P(('dp', 'tensor')), parts along dimension 0, may hold values from 0 to 127, each once within a row
- route_counts: int32 [128], P(('dp', 'tensor')), parts along dimension 0, may hold values from 1 to 64, 256 in all
- w_router: bfloat16 [8192], replicated, may hold values from -0.125 to 0.125
- gain_in: float32 [8192], replicated, may hold values from 0.1 to 1.9
- w_gate_up: bfloat16 [8192, 4096], P(None, 'tensor'), may hold values from -0.0625 to 0.0625
- w_down: bfloat16 [2048, 8192], P('tensor'), may hold values from -0.125 to 0.125
- gain_next: float32 [8192], replicated, may hold values from 0.1 to 1.9
- w_query: bfloat16 [8192, 2048], P(None, 'tensor'), may hold values from -0.0625 to 0.0625
Outputs:
- mixed: bfloat16 [16384, 8192], P(('dp', 'tensor')), parts along dimension 0
- query: bfloat16 [16384, 2048], P('dp', 'tensor'), parts along dimension 0
There are 8 independent parts, one for each index of `dp`. A program takes and returns all parts, laid end to end along the dimension named above; an argument that names none is the same for every part. Nothing has to cross between parts.
Inputs may be any that keep to these rules, and one draw needn't show every extreme that they name: Each row of route_order is a permutation of the owner's local rows 0 to 127. `route_counts`: the counts of one sequence sum to 256; the largest is exactly 64.
All inputs are finite; a program needn't handle non-finite values. No bound on the sum of `route_counts` on one device may be relied on, other than what follows from the above.
Results may differ from a plain program's by a relative error of at most 0.0065.
Values may be sent and summed in bfloat16 or wider, within the bound.
A program may use at most 192 MiB of HBM per device.

v0:
```python
import jax
import jax.numpy as jnp
from jax import lax
from jax.sharding import PartitionSpec as P


def rms_scale(values, gain):
    return values * lax.rsqrt(jnp.mean(values * values, axis=-1, keepdims=True) + 1e-05) * gain


def on_device(
    tokens, route_order, route_counts, w_router, gain_in, w_gate_up, w_down, gain_next, w_query
):
    groups = lax.axis_size("tensor")
    rows_dev = tokens.shape[0]
    route_dev = rows_dev // 8
    slot_count = route_dev * min(4, groups // 2)
    unit_count = w_down.shape[0]
    picked = route_order[0, :slot_count]
    live_count = route_counts[0]
    is_live = jnp.arange(slot_count, dtype=jnp.int32) < live_count
    chosen = tokens[picked]
    chosen_wide = chosen.astype(jnp.float32)
    router_logit = jnp.dot(chosen, w_router, preferred_element_type=jnp.float32)
    normed = jnp.where(is_live[:, None], rms_scale(chosen_wide, gain_in), 0.0).astype(jnp.bfloat16)
    gate_up = jnp.dot(
        lax.all_gather(normed, "tensor", axis=0, tiled=True),
        w_gate_up,
        preferred_element_type=jnp.float32,
    )
    hidden = (jax.nn.silu(gate_up[:, :unit_count]) * gate_up[:, unit_count:]).astype(jnp.bfloat16)
    branch = lax.psum_scatter(
        jnp.dot(hidden, w_down, preferred_element_type=jnp.float32).astype(jnp.bfloat16),
        "tensor",
        scatter_dimension=0,
        tiled=True,
    ).astype(jnp.float32)
    update = (chosen_wide + jax.nn.sigmoid(router_logit)[:, None] * branch).astype(jnp.bfloat16)
    update = jnp.where(is_live[:, None], update, chosen)
    mixed = tokens.at[picked].set(update)
    normed_next = rms_scale(mixed.astype(jnp.float32), gain_next).astype(jnp.bfloat16)
    query = jnp.dot(
        lax.all_gather(normed_next, "tensor", axis=0, tiled=True),
        w_query,
        preferred_element_type=jnp.float32,
    ).astype(jnp.bfloat16)
    return (mixed, query)


def solution(mesh):
    in_specs = (
        P(("dp", "tensor"), None),
        P(("dp", "tensor"), None),
        P(("dp", "tensor")),
        P(),
        P(),
        P(None, "tensor"),
        P("tensor", None),
        P(),
        P(None, "tensor"),
    )
    out_specs = (P(("dp", "tensor"), None), P("dp", "tensor"))
    return jax.shard_map(
        on_device, mesh=mesh, in_specs=in_specs, out_specs=out_specs, check_vma=False
    )
```

profile of v0, /device:TPU:1, one launch (start us, length us, event | category | flops | bytes accessed | tf_op | source)
XLA Modules:
  0.0 490.8 jit_solution(8580013175159059895)
XLA Ops:
  7.2 0.0 copy-start
  7.2 0.0 copy-start.7
  7.2 0.0 all-gather.3.cloned.1.call-start
  7.2 3.2 copy.14
  11.1 0.0 copy-done.7
  11.2 0.0 copy-start.4
  11.2 4.0 gather_fusion
  15.2 0.3 fusion.3
  15.5 0.0 copy-done.4
  15.5 1.4 fusion.6
  16.9 0.0 all-gather.3.cloned.1.call-update
  16.9 0.0 reduce-scatter.2.cloned.1.call-start
  17.0 114.7 %all-gather.3.cloned.1.call-done = bf16[1024,8192]{1,0:T(8,128)(2,1)} async-done(((bf16[64,8192]{1,0:T(8,128)(2,1)}), bf16[1024,8192]{1,0:T(8,128)(2,1)}) %all-gather.3.cloned.1.call-update) | async-done | bytes 16777232 | tf_op jit(solution)/shard_map/all_gather | solution.py:27
  131.7 12.4 %fusion.22 = f32[1024,256]{1,0:T(8,128)} fusion(bf16[1024,8192]{1,0:T(8,128)(2,1)} %all-gather.3.cloned.1.call-done, bf16[8192,256]{1,0:T(8,128)(2,1)} %param.14), kind=kOutput, calls=%fused_computation.36 | convolution fusion | flops 4294967296 | bytes 22020096 | tf_op jit(solution)/shard_map/dot_general | solution.py:26
  144.1 0.0 copy-done
  144.1 9.3 %convolution_convert_fusion = bf16[1024,8192]{1,0:T(8,128)(2,1)} fusion(bf16[128,8192]{1,0:T(8,128)(2,1)S(1)} %copy-done, f32[1024,256]{1,0:T(8,128)} %fusion.22), kind=kOutput, calls=%fused_computation.2 | convolution fusion | flops 2156658688 | bytes 19922944 | tf_op jit(solution)/shard_map/dot_general | solution.py:33
  153.5 0.0 reduce-scatter.2.cloned.1.call-update
  153.5 0.0 all-gather.5.cloned.1.call-start
  153.6 0.6 copy-done.6
  154.2 0.4 fusion.12
  154.6 109.0 %reduce-scatter.2.cloned.1.call-done = bf16[64,8192]{1,0:T(8,128)(2,1)} async-done(((bf16[1024,8192]{1,0:T(8,128)(2,1)}), bf16[64,8192]{1,0:T(8,128)(2,1)}) %reduce-scatter.2.cloned.1.call-update) | async-done | bytes 1048592 | tf_op jit(solution)/shard_map/reduce_scatter | solution.py:32
  263.6 0.0 copy-done.2
  263.6 4.3 scatter_custom_fusion
  267.8 0.0 copy-start.3
  267.8 0.0 copy-start.5
  267.9 0.5 fusion
  268.4 0.3 copy-done.5
  268.6 1.9 fusion.2
  270.5 0.0 copy-done.3
  270.5 0.0 all-gather.5.cloned.1.call-update
  270.6 197.3 %all-gather.5.cloned.1.call-done = bf16[2048,8192]{1,0:T(8,128)(2,1)} async-done(((bf16[128,8192]{1,0:T(8,128)(2,1)}), bf16[2048,8192]{1,0:T(8,128)(2,1)}) %all-gather.5.cloned.1.call-update) | async-done | bytes 33554448 | tf_op jit(solution)/shard_map/all_gather | solution.py:43
  467.8 16.5 %convolution_convert_fusion.1 = bf16[2048,128]{1,0:T(8,128)(2,1)} fusion(bf16[2048,8192]{1,0:T(8,128)(2,1)} %all-gather.5.cloned.1.call-done, bf16[8192,128]{1,0:T(8,128)(2,1)} %param.17), kind=kOutput, calls=%fused_computation.11 | convolution fusion | flops 4295229440 | bytes 36175872 | tf_op jit(solution)/shard_map/dot_general | solution.py:42
  (10 shorter events, 0.1 us)
Async XLA Ops:
  7.2 137.0 %copy-start = (bf16[128,8192]{1,0:T(8,128)(2,1)S(1)}, bf16[128,8192]{1,0:T(8,128)(2,1)}, u32[]{:S(2)}) copy-start(bf16[128,8192]{1,0:T(8,128)(2,1)} %param.15) | copy-start | bytes 6291460
  7.2 4.0 copy-start.7
  7.2 124.5 %all-gather.3.cloned.1.call-start = ((), (), s32[]{:S(2)}) async-start(), calls=%async_computation.1 | async-start | bytes 17825792 | tf_op jit(solution)/shard_map/all_gather | solution.py:27
  11.2 4.4 copy-start.4
  16.9 246.6 %reduce-scatter.2.cloned.1.call-start = ((), (), s32[]{:S(2)}) async-start(), calls=%async_computation.2 | async-start | bytes 17825792 | tf_op jit(solution)/shard_map/reduce_scatter | solution.py:32
  153.5 0.7 copy-start.6
  153.5 110.1 %copy-start.2 = (bf16[128,8192]{1,0:T(8,128)(2,1)S(1)}, bf16[128,8192]{1,0:T(8,128)(2,1)}, u32[]{:S(2)}) copy-start(bf16[128,8192]{1,0:T(8,128)(2,1)} %copy.14) | copy-start | bytes 6291460
  153.5 314.3 %all-gather.5.cloned.1.call-start = ((), (), s32[]{:S(2)}) async-start(), calls=%async_computation.3 | async-start | bytes 35651584 | tf_op jit(solution)/shard_map/all_gather | solution.py:43
  267.8 2.7 copy-start.3
  267.8 0.8 copy-start.5
  467.8 16.5 %copy-start.1 = (bf16[128,8192]{1,0:T(8,128)(2,1)S(1)}, bf16[128,8192]{1,0:T(8,128)(2,1)}, u32[]{:S(2)}) copy-start(bf16[128,8192]{1,0:T(8,128)(2,1)} %param.15) | copy-start | bytes 6291460
Sparse Core Ops, SparseCore 0:
  17.0 114.6 all-gather.2
  153.6 109.8 reduce-scatter.1
  270.7 197.0 all-gather.4
where the time goes:
time: 491 us
  waiting for transfers between devices  421 us (86%)
  matrix products  38.6 us (8%)
  between operations  14.5 us (3%)
  other arithmetic  8.36 us (2%)
  local copies, waits for them, and re-layouts  8.22 us (2%)
    all_gather x1, waiting for transfers between devices, on_device(): lax.all_gather(normed_next, 'tensor', axis=0, tiled=True)  197 us
    all_gather x1, waiting for transfers between devices, on_device(): lax.all_gather(normed, 'tensor', axis=0, tiled=True)  115 us
    reduce_scatter x1, waiting for transfers between devices, on_device(): lax.psum_scatter(jnp.dot(hidden, w_down, preferred_element_type=jnp.float...  109 us
    dot_general x1, matrix products, on_device(): jnp.dot(lax.all_gather(normed_next, 'tensor', axis=0, tiled=True), w_quer...  16.5 us
    dot_general x1, matrix products, on_device(): jnp.dot(lax.all_gather(normed, 'tensor', axis=0, tiled=True), w_gate_up,...  12.4 us
  transfers between devices with their start and end apart: 3, of which 3 were waited for; matrix products, arithmetic and copies ran while one was open for 0% of the time, Pallas kernels for 0%

commit v1 on v0

v1 whole, which is shorter than its diff:
```python
import jax
import jax.numpy as jnp
from jax import lax
from jax.experimental import pallas as pl
from jax.experimental.pallas import tpu as pltpu
from jax.sharding import PartitionSpec as P

T = 16
DP = 8
D = 8192
ROWS = 128
HEAD = 128
UNITS = 128
QN = 4
CW = D // QN
KE = D // DP
ROUTED = 256
BAL = ROUTED // T
EPS = 1e-05
MESH = pl.DeviceIdType.MESH
BF = jnp.bfloat16
F32 = jnp.float32
I32 = jnp.int32


def spread(axis, size, me, source, target, send_sem, recv_sem):
    def body(k, carry):
        peer = lax.rem(me + k, size)
        pltpu.make_async_remote_copy(
            src_ref=source(peer),
            dst_ref=target,
            send_sem=send_sem,
            recv_sem=recv_sem,
            device_id={axis: peer},
            device_id_type=MESH,
        ).start()
        return carry

    lax.fori_loop(1, size, body, 0)


def drain(view, sem):
    pltpu.make_async_copy(view, view, sem).wait()


def iota(shape, dim):
    return lax.broadcasted_iota(I32, shape, dim)


def dot(a, b):
    return jnp.dot(a, b, preferred_element_type=F32)


def one_hot(mask):
    return jnp.where(mask, 1.0, 0.0).astype(BF)


def column_of(row):
    eye = iota((ROWS, ROWS), 0) == iota((ROWS, ROWS), 1)
    return jnp.sum(jnp.where(eye, row.astype(F32), 0.0), axis=1, keepdims=True).astype(I32)


def kernel(
    order_ref, count_ref, wr_ref, gin_ref, gnx_ref, tok_hbm, wgu_hbm, wd_hbm, wq_hbm,
    mixed_hbm, query_hbm,
    tok, wgu, wd, tabs, offs, n0, xr, wqg, pq, qr, a2s, a2r, ag, part, rs, xb,
    rts, rtr, nn, nr, rp, rpr, rqs, rq, q0s, q0r, mix, qo,
    local_sem, send_sem, recv_sem,
):
    t = lax.axis_index("tensor")
    d = lax.axis_index("dp")

    load_tok = pltpu.make_async_copy(tok_hbm, tok, local_sem.at[0])
    load_tok.start()
    load_wgu = pltpu.make_async_copy(wgu_hbm, wgu, local_sem.at[1])
    load_wgu.start()
    load_wd = pltpu.make_async_copy(wd_hbm, wd, local_sem.at[2])
    load_wd.start()

    def wq_rows(peer_d):
        return wq_hbm.at[pl.ds(pl.multiple_of(peer_d * KE, KE), KE), :]

    def wq_cols(at):
        return wqg.at[:, pl.ds(pl.multiple_of(at * HEAD, HEAD), HEAD)]

    own_wq = pltpu.make_async_copy(wq_rows(d), wq_cols(t), local_sem.at[3])
    own_wq.start()

    barrier = pltpu.get_barrier_semaphore()

    def greet_t(k, carry):
        pl.semaphore_signal(barrier, inc=1, device_id={"tensor": lax.rem(t + k, T)}, device_id_type=MESH)
        return carry

    def greet_d(k, carry):
        pl.semaphore_signal(barrier, inc=1, device_id={"dp": lax.rem(d + k, DP)}, device_id_type=MESH)
        return carry

    lax.fori_loop(1, T, greet_t, 0)
    lax.fori_loop(1, DP, greet_d, 0)
    pl.semaphore_wait(barrier, T - 1 + DP - 1)

    count = count_ref[0]
    slot = iota((8, ROWS), 1)
    values = jnp.where(slot < count, slot + 1, 0).astype(F32).astype(BF)
    pairs = one_hot(iota((ROWS, ROWS), 0) == order_ref[...])
    own = lax.dot_general(values, pairs, (((1,), (1,)), ((), ())), preferred_element_type=F32)
    tabs[pl.ds(t, 1)] = (own.astype(I32) - 1)[None]
    spread("tensor", T, t, lambda peer: tabs.at[t], tabs.at[t], send_sem.at[0], recv_sem.at[0])

    load_tok.wait()
    square = jnp.zeros((ROWS, 1), F32)
    for e in range(DP):
        wide = tok[:, e * KE:(e + 1) * KE].astype(F32)
        square += jnp.sum(wide * wide, axis=1, keepdims=True)
    scale = lax.rsqrt(square / D + EPS)
    for e in range(DP):
        cols = slice(e * KE, (e + 1) * KE)
        n0[e] = (tok[:, cols].astype(F32) * scale * gnx_ref[:, cols]).astype(BF)
    spread("dp", DP, d, lambda peer: n0.at[peer], xr.at[d], send_sem.at[1], recv_sem.at[1])
    own_n0 = pltpu.make_async_copy(n0.at[d], xr.at[d], local_sem.at[4])
    own_n0.start()

    drain(tabs.at[pl.ds(0, T - 1)], recv_sem.at[0])
    marks = one_hot(tabs[...].reshape(T * 8, ROWS) >= 0)
    counts = dot(marks, jnp.ones((ROWS, ROWS), BF))
    sub, lane = iota((ROWS, ROWS), 0), iota((ROWS, ROWS), 1)
    before = one_hot(((lane // 8) < (sub // 8)) & (lane % 8 == 0))
    firsts = dot(before, counts.astype(BF))
    firsts_i, counts_i = firsts.astype(I32), counts.astype(I32)
    offs[...] = firsts_i
    first_l, last_l = [], []
    for half in range(2):
        group = iota((8, ROWS), 1) // 16
        lo, hi = jnp.zeros((8, ROWS), I32), jnp.zeros((8, ROWS), I32)
        for i in range(8):
            o = half * 8 + i
            f = firsts_i[o * 8:(o + 1) * 8]
            c = counts_i[o * 8:(o + 1) * 8]
            lo = jnp.where(group == i, f, lo)
            hi = jnp.where(group == i, f + c, hi)
        first_l.append(lo)
        last_l.append(hi)
    first_l = jnp.concatenate(first_l, axis=1)[:1]
    last_l = jnp.concatenate(last_l, axis=1)[:1]

    my_first = offs[pl.ds(pl.multiple_of(t * 8, 8), 8), :][:1]
    my_slots = tabs[pl.ds(t, 1)][0, :1]
    g_row = jnp.where(my_slots >= 0, my_slots + my_first, -1)
    j = iota((ROUTED, ROWS), 0)
    hit = ((j // 16) == (g_row % 16)) & ((j % 4) == ((g_row // 16) % 4)) & (g_row >= 0)
    pick = jnp.concatenate([one_hot(hit & (((j // 4) % 4) == q)) for q in range(QN)], axis=1)
    tile = 512
    for i in range(CW // tile):
        stacked = jnp.concatenate([tok[:, q * CW + i * tile:q * CW + (i + 1) * tile] for q in range(QN)], axis=0)
        a2s[:, i * tile:(i + 1) * tile] = dot(pick, stacked).astype(BF)

    def block16(ref, at):
        return ref.at[pl.ds(pl.multiple_of(at * 16, 16), 16), :]

    spread("tensor", T, t, lambda peer: block16(a2s, peer), block16(a2r, t), send_sem.at[2], recv_sem.at[2])
    own_a2 = pltpu.make_async_copy(block16(a2s, t), block16(a2r, t), local_sem.at[5])
    own_a2.start()

    spread("tensor", T, t, lambda peer: wq_rows(d), wq_cols(t), send_sem.at[3], recv_sem.at[3])

    bi, bj = iota((QN * BAL, ROUTED), 0), iota((QN * BAL, ROUTED), 1)
    g_bal = (bi % BAL) * T + t
    compact = one_hot(
        ((bi // BAL) == ((bj // 4) % 4)) & ((bj % 4) == (bi % 4)) & (first_l <= g_bal) & (g_bal < last_l)
    )
    own_a2.wait()
    drain(a2r.at[pl.ds(0, (T - 1) * 16), :], recv_sem.at[2])
    square, logit = jnp.zeros((BAL, 1), F32), jnp.zeros((BAL, 1), F32)
    xb[...] = dot(compact, a2r[...])
    for q in range(QN):
        rows = xb[q * BAL:(q + 1) * BAL]
        square += jnp.sum(rows * rows, axis=1, keepdims=True)
        logit += jnp.sum(rows * wr_ref[:, q * CW:(q + 1) * CW].astype(F32), axis=1, keepdims=True)
    scale = lax.rsqrt(square / D + EPS)
    for q in range(QN):
        rows = xb[q * BAL:(q + 1) * BAL] * scale * gin_ref[:, q * CW:(q + 1) * CW]
        ag[q, pl.ds(pl.multiple_of(t * BAL, BAL), BAL), :] = rows.astype(BF)

    def ag_block(ref, at):
        return ref.at[:, pl.ds(pl.multiple_of(at * BAL, BAL), BAL), :]

    spread("tensor", T, t, lambda peer: ag_block(ag, t), ag_block(ag, t), send_sem.at[4], recv_sem.at[4])

    own_n0.wait()
    own_wq.wait()
    drain(xr.at[pl.ds(0, DP - 1)], recv_sem.at[1])
    drain(wqg.at[:, pl.ds(0, (T - 1) * HEAD)], recv_sem.at[3])

    def query_tile(i, carry):
        cols = pl.ds(pl.multiple_of(i * 256, 256), 256)
        weights = wqg[:, cols]
        for e in range(DP):
            pq[e, :, cols] = dot(xr[e], weights).astype(BF)
        return carry

    lax.fori_loop(0, T * HEAD // 256, query_tile, 0)
    spread("dp", DP, d, lambda peer: pq.at[peer], qr.at[d], send_sem.at[5], recv_sem.at[5])
    own_pq = pltpu.make_async_copy(pq.at[d], qr.at[d], local_sem.at[6])
    own_pq.start()

    load_wgu.wait()
    load_wd.wait()
    drain(ag.at[:, pl.ds(0, (T - 1) * BAL), :], recv_sem.at[4])
    gate_up = dot(ag[0], wgu[:CW])
    for q in range(1, QN):
        gate_up += dot(ag[q], wgu[q * CW:(q + 1) * CW])
    gate, up = gate_up[:, :UNITS], gate_up[:, UNITS:]
    hidden = (gate / (1.0 + jnp.exp(-gate)) * up).astype(BF)
    for q in range(QN):
        for i in range(CW // tile):
            at = q * CW + i * tile
            part[q, :, i * tile:(i + 1) * tile] = dot(hidden, wd[:, at:at + tile]).astype(BF)
    spread("tensor", T, t, lambda peer: ag_block(part, peer), rs.at[t], send_sem.at[6], recv_sem.at[6])
    own_part = pltpu.make_async_copy(ag_block(part, t), rs.at[t], local_sem.at[7])
    own_part.start()

    own_pq.wait()
    drain(qr.at[pl.ds(0, DP - 1)], recv_sem.at[5])

    def head_tile(i, carry):
        cols = pl.ds(pl.multiple_of(i * HEAD, HEAD), HEAD)
        total = qr[0, :, cols].astype(F32)
        for e in range(1, DP):
            total += qr[e, :, cols].astype(F32)
        q0s[pl.ds(i, 1)] = total.astype(BF)[None]
        return carry

    lax.fori_loop(0, T, head_tile, 0)
    spread("tensor", T, t, lambda peer: q0s.at[peer], q0r.at[t], send_sem.at[7], recv_sem.at[7])
    own_q0 = pltpu.make_async_copy(q0s.at[t], q0r.at[t], local_sem.at[8])
    own_q0.start()

    own_part.wait()
    drain(rs.at[pl.ds(0, T - 1)], recv_sem.at[6])
    weight = 1.0 / (1.0 + jnp.exp(-logit))
    square = jnp.zeros((BAL, 1), F32)
    mixed_b = []
    for q in range(QN):
        branch = rs[0, q].astype(F32)
        for s in range(1, T):
            branch += rs[s, q].astype(F32)
        rows = (xb[q * BAL:(q + 1) * BAL] + weight * branch).astype(BF)
        mixed_b.append(rows)
        wide = rows.astype(F32)
        square += jnp.sum(wide * wide, axis=1, keepdims=True)
    scale = lax.rsqrt(square / D + EPS)
    for q in range(QN):
        wide = mixed_b[q].astype(F32) * scale * gnx_ref[:, q * CW:(q + 1) * CW]
        for h in range(CW // KE):
            nn[q * (CW // KE) + h] = wide[:, h * KE:(h + 1) * KE].astype(BF)
    spread("dp", DP, d, lambda peer: nn.at[peer], nr.at[d], send_sem.at[8], recv_sem.at[8])
    own_nn = pltpu.make_async_copy(nn.at[d], nr.at[d], local_sem.at[9])
    own_nn.start()

    stacked = jnp.concatenate(mixed_b, axis=0)
    ri, rj = iota((16, QN * BAL), 0), iota((16, QN * BAL), 1)
    g_bal = (rj % BAL) * T + t
    fits = ((rj // BAL) == (ri // 4)) & ((rj % 4) == (ri % 4))
    back = []
    for o in range(T):
        lo = jnp.concatenate([firsts_i[o * 8:(o + 1) * 8, :QN * BAL]] * 2, axis=0)
        n = jnp.concatenate([counts_i[o * 8:(o + 1) * 8, :QN * BAL]] * 2, axis=0)
        back.append(one_hot(fits & (lo <= g_bal) & (g_bal < lo + n)))
    back = jnp.concatenate(back, axis=0)
    for i in range(CW // tile):
        rts[:, i * tile:(i + 1) * tile] = dot(back, stacked[:, i * tile:(i + 1) * tile]).astype(BF)
    spread("tensor", T, t, lambda peer: block16(rts, peer), block16(rtr, t), send_sem.at[9], recv_sem.at[9])
    own_rt = pltpu.make_async_copy(block16(rts, t), block16(rtr, t), local_sem.at[10])
    own_rt.start()

    own_nn.wait()
    drain(nr.at[pl.ds(0, DP - 1)], recv_sem.at[8])
    rows = nr[...].reshape(DP * BAL, KE)
    for i in range(T * HEAD // tile):
        cols = slice(i * tile, (i + 1) * tile)
        rp[:, :, cols] = dot(rows, wqg[:, cols]).astype(BF).reshape(DP, BAL, tile)
    spread("dp", DP, d, lambda peer: rp.at[peer], rpr.at[d], send_sem.at[10], recv_sem.at[10])
    own_rp = pltpu.make_async_copy(rp.at[d], rpr.at[d], local_sem.at[11])
    own_rp.start()

    own_rp.wait()
    drain(rpr.at[pl.ds(0, DP - 1)], recv_sem.at[10])
    total = rpr[0].astype(F32)
    for e in range(1, DP):
        total += rpr[e].astype(F32)
    total = total.astype(BF)
    for h in range(T):
        rqs[h] = total[:, h * HEAD:(h + 1) * HEAD]
    spread("tensor", T, t, lambda peer: rqs.at[peer], rq.at[t], send_sem.at[11], recv_sem.at[11])
    own_rq = pltpu.make_async_copy(rqs.at[t], rq.at[t], local_sem.at[12])
    own_rq.start()

    own_rt.wait()
    drain(rtr.at[pl.ds(0, (T - 1) * 16), :], recv_sem.at[9])
    g_col = column_of(g_row)
    jl = iota((ROWS, ROUTED), 1)
    hit = ((jl // 16) == (g_col % 16)) & ((jl % 4) == ((g_col // 16) % 4)) & (g_col >= 0)
    for q in range(QN):
        place = one_hot(hit & (((jl // 4) % 4) == q))
        for i in range(CW // tile):
            at = q * CW + i * tile
            moved = dot(place, rtr[:, i * tile:(i + 1) * tile]).astype(BF)
            mix[:, at:at + tile] = jnp.where(g_col >= 0, moved, tok[:, at:at + tile])
    out_mixed = pltpu.make_async_copy(mix, mixed_hbm, local_sem.at[13])
    out_mixed.start()

    own_q0.wait()
    drain(q0r.at[pl.ds(0, T - 1)], recv_sem.at[7])
    own_rq.wait()
    drain(rq.at[pl.ds(0, T - 1)], recv_sem.at[11])
    routed = rq[...].reshape(ROUTED, HEAD)
    g_lane = (jl % 16) * T + jl // 16

    def place_owner(o, carry):
        slots = tabs[pl.ds(o, 1)][0, :1]
        lo = offs[pl.ds(pl.multiple_of(o * 8, 8), 8), :][:1]
        col = column_of(jnp.where(slots >= 0, slots + lo, -1))
        moved = dot(one_hot(col == g_lane), routed).astype(BF)
        plain = q0r[pl.ds(o, 1)][0]
        qo[pl.ds(pl.multiple_of(o * ROWS, ROWS), ROWS), :] = jnp.where(col >= 0, moved, plain)
        return carry

    lax.fori_loop(0, T, place_owner, 0)
    out_query = pltpu.make_async_copy(qo, query_hbm, local_sem.at[14])
    out_query.start()

    drain(tabs.at[pl.ds(0, T - 1)], send_sem.at[0])
    drain(n0.at[pl.ds(0, DP - 1)], send_sem.at[1])
    drain(a2s.at[pl.ds(0, (T - 1) * 16), :], send_sem.at[2])
    drain(wqg.at[:, pl.ds(0, (T - 1) * HEAD)], send_sem.at[3])
    drain(ag.at[:, pl.ds(0, (T - 1) * BAL), :], send_sem.at[4])
    drain(pq.at[pl.ds(0, DP - 1)], send_sem.at[5])
    drain(part.at[:, pl.ds(0, (T - 1) * BAL), :], send_sem.at[6])
    drain(q0s.at[pl.ds(0, T - 1)], send_sem.at[7])
    drain(nn.at[pl.ds(0, DP - 1)], send_sem.at[8])
    drain(rts.at[pl.ds(0, (T - 1) * 16), :], send_sem.at[9])
    drain(rp.at[pl.ds(0, DP - 1)], send_sem.at[10])
    drain(rqs.at[pl.ds(0, T - 1)], send_sem.at[11])
    out_mixed.wait()
    out_query.wait()


def on_device(tokens, route_order, route_counts, w_router, gain_in, w_gate_up, w_down, gain_next, w_query):
    vmem = pl.BlockSpec(memory_space=pltpu.VMEM)
    anywhere = pl.BlockSpec(memory_space=pl.ANY)
    return pl.pallas_call(
        kernel,
        out_shape=(
            jax.ShapeDtypeStruct((ROWS, D), BF),
            jax.ShapeDtypeStruct((T * ROWS, HEAD), BF),
        ),
        in_specs=[vmem, pl.BlockSpec(memory_space=pltpu.SMEM), vmem, vmem, vmem] + [anywhere] * 4,
        out_specs=(anywhere, anywhere),
        scratch_shapes=[
            pltpu.VMEM((ROWS, D), BF),
            pltpu.VMEM((D, 2 * UNITS), BF),
            pltpu.VMEM((UNITS, D), BF),
            pltpu.VMEM((T, 8, ROWS), I32),
            pltpu.VMEM((ROWS, ROWS), I32),
            pltpu.VMEM((DP, ROWS, KE), BF),
            pltpu.VMEM((DP, ROWS, KE), BF),
            pltpu.VMEM((KE, T * HEAD), BF),
            pltpu.VMEM((DP, ROWS, T * HEAD), BF),
            pltpu.VMEM((DP, ROWS, T * HEAD), BF),
            pltpu.VMEM((ROUTED, CW), BF),
            pltpu.VMEM((ROUTED, CW), BF),
            pltpu.VMEM((QN, ROUTED, CW), BF),
            pltpu.VMEM((QN, ROUTED, CW), BF),
            pltpu.VMEM((T, QN, BAL, CW), BF),
            pltpu.VMEM((QN * BAL, CW), F32),
            pltpu.VMEM((ROUTED, CW), BF),
            pltpu.VMEM((ROUTED, CW), BF),
            pltpu.VMEM((DP, BAL, KE), BF),
            pltpu.VMEM((DP, BAL, KE), BF),
            pltpu.VMEM((DP, BAL, T * HEAD), BF),
            pltpu.VMEM((DP, BAL, T * HEAD), BF),
            pltpu.VMEM((T, BAL, HEAD), BF),
            pltpu.VMEM((T, BAL, HEAD), BF),
            pltpu.VMEM((T, ROWS, HEAD), BF),
            pltpu.VMEM((T, ROWS, HEAD), BF),
            pltpu.VMEM((ROWS, D), BF),
            pltpu.VMEM((T * ROWS, HEAD), BF),
            pltpu.SemaphoreType.DMA((15,)),
            pltpu.SemaphoreType.DMA((12,)),
            pltpu.SemaphoreType.DMA((12,)),
        ],
        compiler_params=pltpu.CompilerParams(
            collective_id=0, has_side_effects=True, vmem_limit_bytes=60 * 1024 * 1024
        ),
    )(
        route_order, route_counts, w_router.reshape(1, D), gain_in.reshape(1, D), gain_next.reshape(1, D),
        tokens, w_gate_up, w_down, w_query,
    )


def solution(mesh):
    in_specs = (
        P(("dp", "tensor"), None),
        P(("dp", "tensor"), None),
        P(("dp", "tensor")),
        P(),
        P(),
        P(None, "tensor"),
        P("tensor", None),
        P(),
        P(None, "tensor"),
    )
    out_specs = (P(("dp", "tensor"), None), P("dp", "tensor"))
    return jax.shard_map(
        on_device, mesh=mesh, in_specs=in_specs, out_specs=out_specs, check_vma=False
    )
```

time: 491 us -> 247 us (0.50)
  waiting for transfers between devices: 421 us -> 0 us
  Pallas kernels: 0 us -> 240 us
  matrix products: 38.6 us -> 0 us
  between operations: 14.5 us -> 1.29 us
  other arithmetic: 8.36 us -> 0 us
    all_gather x2 -> x0, waiting for transfers between devices: 312 us -> none  [the longest x1 197 us: on_device(): lax.all_gather(normed_next, 'tensor', axis=0, tiled=True)]
    pallas_call x0 -> x1, Pallas kernels: none -> 240 us  [on_device(): pl.pallas_call(kernel, out_shape=(jax.ShapeDtypeStruct((ROWS, D), BF), ja...]
    reduce_scatter x1 -> x0, waiting for transfers between devices: 109 us -> none  [on_device(): lax.psum_scatter(jnp.dot(hidden, w_down, preferred_element_type=jnp.float...]
    dot_general x4 -> x0, matrix products: 38.6 us -> none  [the longest x1 16.5 us: on_device(): jnp.dot(lax.all_gather(normed_next, 'tensor', axis=0, tiled=True), w_quer...]
  transfers between devices with their start and end apart: 3 -> 0, of which waited for: 3 -> 0; matrix products, arithmetic and copies ran while one was open for 0% -> 0% of each run, Pallas kernels for 0% -> 0%
where the time goes in v1:
time: 247 us
  Pallas kernels  240 us (97%)
  local copies, waits for them, and re-layouts  5.3 us (2%)
    pallas_call x1, Pallas kernels, on_device(): pl.pallas_call(kernel, out_shape=(jax.ShapeDtypeStruct((ROWS, D), BF), ja...  240 us

profile of v1, /device:TPU:1, one launch (start us, length us, event | category | flops | bytes accessed | tf_op | source)
XLA Modules:
  0.0 246.9 jit_solution(15107889403977274611)
XLA Ops:
  1.3 1.4 reshape.13.wr_ref
  2.6 240.3 %shard_map.104 = (bf16[128,8192]{1,0:T(8,128)(2,1)}, bf16[2048,128]{1,0:T(8,128)(2,1)}) custom-call(s32[1,128]{1,0:T(1,128)} %order_ref.1, s32[1]{0:T(128)S(6)} %copy.13.count_ref, bf16[1,8192]{1,0:T(2,128)(2,1)} %reshape.13.wr_ref, f32[1,8192]{1,0:T(1,128)} %bitcast.2, f32[1,8192]{1,0:T(1,128)} %bitcast.3, bf16[128,8192]{1,0:T(8,128)(2,1)} %tok_hbm.1, ...), custom_call_target="tpu_custom_call" | custom-call | tf_op jit(solution)/shard_map/pallas_call | solution.py:352
  243.0 0.0 copy-start
  243.0 3.2 %copy.14 = bf16[128,8192]{1,0:T(8,128)(2,1)} copy(bf16[128,8192]{1,0:T(8,128)(2,1)} %get-tuple-element.4) | data formatting | bytes 4194304
  246.1 0.0 copy-done
  246.1 0.8 copy.15
Async XLA Ops:
  243.0 3.2 %copy-start = (bf16[2048,128]{1,0:T(8,128)(2,1)S(1)}, bf16[2048,128]{1,0:T(8,128)(2,1)}, u32[]{:S(2)}) copy-start(bf16[2048,128]{1,0:T(8,128)(2,1)} %get-tuple-element.5) | copy-start | bytes 1572868

commit v2 on v1

v2 whole, which is shorter than its diff:
```python
import jax
import jax.numpy as jnp
from jax import lax
from jax.experimental import pallas as pl
from jax.experimental.pallas import tpu as pltpu
from jax.sharding import PartitionSpec as P

T = 16
DP = 8
D = 8192
ROWS = 128
HEAD = 128
UNITS = 128
QN = 4
CW = D // QN
KE = D // DP
ROUTED = 256
BAL = ROUTED // T
NZ = 4
NY = 4
NX = 4
NC = 2
LINE = DP * BAL
HALF = KE // 2
EPS = 1e-05
MESH = pl.DeviceIdType.MESH
BF = jnp.bfloat16
F32 = jnp.float32
I32 = jnp.int32


def start(source, target, axis, peer, send_sem, recv_sem):
    pltpu.make_async_remote_copy(
        src_ref=source,
        dst_ref=target,
        send_sem=send_sem,
        recv_sem=recv_sem,
        device_id={axis: peer},
        device_id_type=MESH,
    ).start()


def spread(axis, size, me, source, target, send_sem, recv_sem):
    def body(k, carry):
        peer = lax.rem(me + k, size)
        start(source(peer), target, axis, peer, send_sem, recv_sem)
        return carry

    lax.fori_loop(1, size, body, 0)


def drain(view, sem):
    pltpu.make_async_copy(view, view, sem).wait()


def iota(shape, dim):
    return lax.broadcasted_iota(I32, shape, dim)


def dot(a, b):
    return jnp.dot(a, b, preferred_element_type=F32)


def one_hot(mask):
    return jnp.where(mask, 1.0, 0.0).astype(BF)


def aligned(at, size):
    return pl.ds(pl.multiple_of(at * size, size), size)


def column_of(row):
    eye = iota((ROWS, ROWS), 0) == iota((ROWS, ROWS), 1)
    return jnp.sum(jnp.where(eye, row.astype(F32), 0.0), axis=1, keepdims=True).astype(I32)


def kernel(
    order_ref, count_ref, wr_ref, gin_ref, gnx_ref, tok_hbm, wgu_hbm, wd_hbm, wq_hbm,
    mixed_hbm, query_hbm,
    tok, tabs, offs, n0, xr, wga, wda, wqa, wqb, a2s, a2r, xb, ns, gx, rws, rwr,
    gp, gc, gs, gr, hid, dn, dr, pq, pc, ps, qr, q0s, q0r, ms, mb, rp, rpr, rqs, rq,
    rts, rtr, mix, qo,
    local_sem, send_sem, recv_sem,
):
    t = lax.axis_index("tensor")
    d = lax.axis_index("dp")
    z, y = lax.div(t, NY), lax.rem(t, NY)
    x, c = lax.div(d, NC), lax.rem(d, NC)
    near = (1, 3, 2)

    def at_y(k):
        return lax.rem(y + k, NY)

    def at_z(k):
        return lax.rem(z + k, NZ)

    def at_x(k):
        return lax.rem(x + k, NX)

    my_k = aligned(d, KE)
    load_tok = pltpu.make_async_copy(tok_hbm, tok, local_sem.at[0])
    load_tok.start()
    own_wg = pltpu.make_async_copy(wgu_hbm.at[my_k, :], wga.at[y], local_sem.at[1])
    own_wg.start()
    own_wd = pltpu.make_async_copy(wd_hbm.at[:, my_k], wda.at[y], local_sem.at[2])
    own_wd.start()

    def wq_half(i):
        return wq_hbm.at[pl.ds(pl.multiple_of(d * KE + i * HALF, HALF), HALF), :]

    own_wqa = pltpu.make_async_copy(wq_half(0), wqa.at[:, aligned(z * NY + y, HEAD)], local_sem.at[3])
    own_wqa.start()
    own_wqb = pltpu.make_async_copy(wq_half(1), wqb.at[:, aligned(y * NZ + z, HEAD)], local_sem.at[4])
    own_wqb.start()

    barrier = pltpu.get_barrier_semaphore()

    def greet_t(k, carry):
        pl.semaphore_signal(barrier, inc=1, device_id={"tensor": lax.rem(t + k, T)}, device_id_type=MESH)
        return carry

    def greet_d(k, carry):
        pl.semaphore_signal(barrier, inc=1, device_id={"dp": lax.rem(d + k, DP)}, device_id_type=MESH)
        return carry

    lax.fori_loop(1, T, greet_t, 0)
    lax.fori_loop(1, DP, greet_d, 0)
    pl.semaphore_wait(barrier, T - 1 + DP - 1)

    count = count_ref[0]
    slot = iota((8, ROWS), 1)
    values = jnp.where(slot < count, slot + 1, 0).astype(F32).astype(BF)
    pairs = one_hot(iota((ROWS, ROWS), 0) == order_ref[...])
    own = lax.dot_general(values, pairs, (((1,), (1,)), ((), ())), preferred_element_type=F32)
    tabs[pl.ds(t, 1)] = (own.astype(I32) - 1)[None]
    spread("tensor", T, t, lambda peer: tabs.at[t], tabs.at[t], send_sem.at[0], recv_sem.at[0])

    load_tok.wait()
    square = jnp.zeros((ROWS, 1), F32)
    for e in range(DP):
        wide = tok[:, e * KE:(e + 1) * KE].astype(F32)
        square += jnp.sum(wide * wide, axis=1, keepdims=True)
    scale = lax.rsqrt(square / D + EPS)
    for e in range(DP):
        cols = slice(e * KE, (e + 1) * KE)
        n0[e] = (tok[:, cols].astype(F32) * scale * gnx_ref[:, cols]).astype(BF)
    spread("dp", DP, d, lambda peer: n0.at[peer], xr.at[d], send_sem.at[1], recv_sem.at[1])
    own_n0 = pltpu.make_async_copy(n0.at[d], xr.at[d], local_sem.at[5])
    own_n0.start()

    drain(tabs.at[pl.ds(0, T - 1)], recv_sem.at[0])
    marks = one_hot(tabs[...].reshape(T * 8, ROWS) >= 0)
    counts = dot(marks, jnp.ones((ROWS, ROWS), BF))
    sub, lane = iota((ROWS, ROWS), 0), iota((ROWS, ROWS), 1)
    before = one_hot(((lane // 8) < (sub // 8)) & (lane % 8 == 0))
    firsts = dot(before, counts.astype(BF))
    firsts_i, counts_i = firsts.astype(I32), counts.astype(I32)
    offs[...] = firsts_i
    first_l, last_l = [], []
    for half in range(2):
        group = iota((8, ROWS), 1) // 16
        lo, hi = jnp.zeros((8, ROWS), I32), jnp.zeros((8, ROWS), I32)
        for i in range(8):
            o = half * 8 + i
            f = firsts_i[o * 8:(o + 1) * 8]
            n = counts_i[o * 8:(o + 1) * 8]
            lo = jnp.where(group == i, f, lo)
            hi = jnp.where(group == i, f + n, hi)
        first_l.append(lo)
        last_l.append(hi)
    first_l = jnp.concatenate(first_l, axis=1)[:1]
    last_l = jnp.concatenate(last_l, axis=1)[:1]

    my_first = offs[aligned(t, 8), :][:1]
    my_slots = tabs[pl.ds(t, 1)][0, :1]
    g_row = jnp.where(my_slots >= 0, my_slots + my_first, -1)
    j = iota((ROUTED, ROWS), 0)
    hit = ((j // 16) == (g_row % 16)) & ((j % 4) == ((g_row // 16) % 4)) & (g_row >= 0)
    pick = jnp.concatenate([one_hot(hit & (((j // 4) % 4) == q)) for q in range(QN)], axis=1)
    tile = 512
    for i in range(CW // tile):
        stacked = jnp.concatenate([tok[:, q * CW + i * tile:q * CW + (i + 1) * tile] for q in range(QN)], axis=0)
        a2s[:, i * tile:(i + 1) * tile] = dot(pick, stacked).astype(BF)
    spread("tensor", T, t, lambda peer: a2s.at[aligned(peer, 16), :], a2r.at[aligned(t, 16), :], send_sem.at[2], recv_sem.at[2])
    own_a2 = pltpu.make_async_copy(a2s.at[aligned(t, 16), :], a2r.at[aligned(t, 16), :], local_sem.at[6])
    own_a2.start()

    own_wg.wait()
    own_wd.wait()
    own_wqa.wait()
    own_wqb.wait()
    for k in near:
        start(wga.at[y], wga.at[y], "tensor", z * NY + at_y(k), send_sem.at[3], recv_sem.at[3])
    for k in near:
        start(wqb.at[:, aligned(y * NZ + z, HEAD)], wqb.at[:, aligned(y * NZ + z, HEAD)], "tensor", at_z(k) * NY + y, send_sem.at[4], recv_sem.at[4])
    for k in near:
        start(wqa.at[:, aligned(z * NY + y, HEAD)], wqa.at[:, aligned(z * NY + y, HEAD)], "tensor", z * NY + at_y(k), send_sem.at[5], recv_sem.at[5])
    for k in near:
        start(wda.at[y], wda.at[y], "tensor", z * NY + at_y(k), send_sem.at[6], recv_sem.at[6])

    bi, bj = iota((QN * BAL, ROUTED), 0), iota((QN * BAL, ROUTED), 1)
    g_bal = (bi % BAL) * T + t
    compact = one_hot(
        ((bi // BAL) == ((bj // 4) % 4)) & ((bj % 4) == (bi % 4)) & (first_l <= g_bal) & (g_bal < last_l)
    )
    own_a2.wait()
    drain(a2r.at[pl.ds(0, (T - 1) * 16), :], recv_sem.at[2])
    square, logit = jnp.zeros((BAL, 1), F32), jnp.zeros((BAL, 1), F32)
    xb[...] = dot(compact, a2r[...])
    for q in range(QN):
        rows = xb[q * BAL:(q + 1) * BAL]
        square += jnp.sum(rows * rows, axis=1, keepdims=True)
    scale = lax.rsqrt(square / D + EPS)
    per = CW // KE
    for q in range(QN):
        rows = xb[q * BAL:(q + 1) * BAL] * scale * gin_ref[:, q * CW:(q + 1) * CW]
        for h in range(per):
            ns[q * per + h] = rows[:, h * KE:(h + 1) * KE].astype(BF)
    my_rows = gx.at[z, d]
    spread("dp", DP, d, lambda peer: ns.at[peer], my_rows, send_sem.at[7], recv_sem.at[7])
    own_ns = pltpu.make_async_copy(ns.at[d], my_rows, local_sem.at[7])
    own_ns.start()
    for q in range(QN):
        rows = xb[q * BAL:(q + 1) * BAL]
        logit += jnp.sum(rows * wr_ref[:, q * CW:(q + 1) * CW].astype(F32), axis=1, keepdims=True)
        for h in range(per):
            rws[q * per + h, :, :KE] = rows[:, h * KE:(h + 1) * KE].astype(BF)
    weight = 1.0 / (1.0 + jnp.exp(-logit))
    upper = weight.astype(BF)
    lower = (weight - upper.astype(F32)).astype(BF)
    pair = jnp.where(iota((BAL, 128), 1) == 0, upper.astype(F32), lower.astype(F32)).astype(BF)
    for e in range(DP):
        rws[e, :, KE:] = pair
    spread("dp", DP, d, lambda peer: rws.at[peer], rwr.at[d], send_sem.at[8], recv_sem.at[8])
    own_rw = pltpu.make_async_copy(rws.at[d], rwr.at[d], local_sem.at[8])
    own_rw.start()

    own_ns.wait()
    drain(gx.at[0, pl.ds(0, DP - 1)], recv_sem.at[7])
    for k in near:
        start(gx.at[z], gx.at[z], "tensor", at_z(k) * NY + y, send_sem.at[9], recv_sem.at[9])

    drain(wqa.at[:, pl.ds(0, 3 * HEAD)], recv_sem.at[5])
    drain(wqb.at[:, pl.ds(0, 3 * HEAD)], recv_sem.at[4])
    for k in near:
        start(wqa.at[:, aligned(z, NY * HEAD)], wqa.at[:, aligned(z, NY * HEAD)], "tensor", at_z(k) * NY + y, send_sem.at[10], recv_sem.at[10])
        start(wqb.at[:, aligned(y, NZ * HEAD)], wqb.at[:, aligned(y, NZ * HEAD)], "tensor", z * NY + at_y(k), send_sem.at[11], recv_sem.at[11])

    drain(wga.at[pl.ds(0, NY - 1)], recv_sem.at[3])
    drain(gx.at[pl.ds(0, NZ - 1)], recv_sem.at[9])
    rows = gx[...].reshape(NZ * LINE, KE)
    for i in range(NY):
        gp[:, :, :, i * 2 * UNITS:(i + 1) * 2 * UNITS] = dot(rows, wga[i]).reshape(NC, NX, NZ * LINE // DP, 2 * UNITS)
    sibling = x * NC + 1 - c
    start(gp.at[1 - c], gc, "dp", sibling, send_sem.at[12], recv_sem.at[12])
    drain(gc, recv_sem.at[12])
    for i in range(NX):
        gs[i] = (gp[c, i] + gc[i]).astype(BF)
    for k in near:
        start(gs.at[at_x(k)], gr.at[x], "dp", at_x(k) * NC + c, send_sem.at[13], recv_sem.at[13])
    own_gs = pltpu.make_async_copy(gs.at[x], gr.at[x], local_sem.at[9])
    own_gs.start()

    own_gs.wait()
    drain(gr.at[pl.ds(0, NX - 1)], recv_sem.at[13])
    total = gr[0].astype(F32)
    for i in range(1, NX):
        total += gr[i].astype(F32)
    for i in range(NY):
        gate = total[:, i * 2 * UNITS:i * 2 * UNITS + UNITS]
        up = total[:, i * 2 * UNITS + UNITS:(i + 1) * 2 * UNITS]
        hid[c, pl.ds(x, 1), :, i * UNITS:(i + 1) * UNITS] = (gate / (1.0 + jnp.exp(-gate)) * up).astype(BF)[None]
    for k in near:
        start(hid.at[c, x], hid.at[c, x], "dp", at_x(k) * NC + c, send_sem.at[14], recv_sem.at[14])
    drain(hid.at[0, pl.ds(0, NX - 1)], recv_sem.at[14])
    start(hid.at[c], hid.at[c], "dp", sibling, send_sem.at[15], recv_sem.at[15])

    drain(wda.at[pl.ds(0, NY - 1)], recv_sem.at[6])
    drain(hid.at[0], recv_sem.at[15])
    hidden = hid[...].reshape(NZ * LINE, NY * UNITS)
    down = wda[...].reshape(NY * UNITS, KE)
    for i in range(KE // 256):
        cols = slice(i * 256, (i + 1) * 256)
        dn[:, :, cols] = dot(hidden, down[:, cols]).astype(BF).reshape(NZ, LINE, 256)
    for k in near:
        start(dn.at[at_z(k)], dr.at[z], "tensor", at_z(k) * NY + y, send_sem.at[16], recv_sem.at[16])
    own_dn = pltpu.make_async_copy(dn.at[z], dr.at[z], local_sem.at[10])
    own_dn.start()

    own_n0.wait()
    drain(xr.at[pl.ds(0, DP - 1)], recv_sem.at[1])
    drain(wqa.at[:, pl.ds(0, 3 * NY * HEAD)], recv_sem.at[10])
    drain(wqb.at[:, pl.ds(0, 3 * NZ * HEAD)], recv_sem.at[11])

    def head_pair(i):
        hz, hy = lax.div(i, NY // 2), lax.rem(i, NY // 2) * 2
        upper = wqa[:, aligned(i, 2 * HEAD)]
        lower = jnp.concatenate([wqb[:, aligned(hy * NZ + hz, HEAD)], wqb[:, aligned((hy + 1) * NZ + hz, HEAD)]], axis=1)
        return jnp.concatenate([upper, lower], axis=0)

    def query_tile(i, carry):
        weights = head_pair(i)
        for e in range(DP):
            pq[e % NC, e // NC, :, aligned(i, 2 * HEAD)] = dot(xr[e], weights).astype(BF)
        return carry

    lax.fori_loop(0, T // 2, query_tile, 0)
    start(pq.at[1 - c], pc, "dp", sibling, send_sem.at[17], recv_sem.at[17])
    drain(pc, recv_sem.at[17])

    def pair_sum(i, carry):
        cols = aligned(i, 2 * HEAD)
        ps[:, :, cols] = (pq[c, :, :, cols].astype(F32) + pc[:, :, cols].astype(F32)).astype(BF)
        return carry

    lax.fori_loop(0, T // 2, pair_sum, 0)
    for k in near:
        start(ps.at[at_x(k)], qr.at[x], "dp", at_x(k) * NC + c, send_sem.at[18], recv_sem.at[18])
    own_ps = pltpu.make_async_copy(ps.at[x], qr.at[x], local_sem.at[11])
    own_ps.start()

    own_rw.wait()
    drain(rwr.at[pl.ds(0, DP - 1)], recv_sem.at[8])
    own_dn.wait()
    drain(dr.at[pl.ds(0, NZ - 1)], recv_sem.at[16])
    branch = dr[0].astype(F32)
    for i in range(1, NZ):
        branch += dr[i].astype(F32)
    raw = rwr[...].reshape(LINE, KE + 128)
    both = raw[:, KE:].astype(F32)
    weight = both[:, :1] + both[:, 1:2]
    rows = (raw[:, :KE].astype(F32) + weight * branch).astype(BF)
    ms[...] = rows.reshape(DP, BAL, KE)
    spread("dp", DP, d, lambda peer: ms.at[peer], mb.at[d], send_sem.at[19], recv_sem.at[19])
    own_ms = pltpu.make_async_copy(ms.at[d], mb.at[d], local_sem.at[12])
    own_ms.start()
    rows = (rows.astype(F32) * gnx_ref[:, my_k]).astype(BF)
    for i in range(T // 2):
        cols = slice(i * 2 * HEAD, (i + 1) * 2 * HEAD)
        hz, hy = i // (NY // 2), i % (NY // 2) * 2
        first, second = (hy * NZ + hz) * HEAD, ((hy + 1) * NZ + hz) * HEAD
        lower = jnp.concatenate([wqb[:, first:first + HEAD], wqb[:, second:second + HEAD]], axis=1)
        weights = jnp.concatenate([wqa[:, cols], lower], axis=0)
        rp[:, :, cols] = dot(rows, weights).astype(BF).reshape(DP, BAL, 2 * HEAD)
    spread("dp", DP, d, lambda peer: rp.at[peer], rpr.at[d], send_sem.at[20], recv_sem.at[20])
    own_rp = pltpu.make_async_copy(rp.at[d], rpr.at[d], local_sem.at[13])
    own_rp.start()

    own_ms.wait()
    drain(mb.at[pl.ds(0, DP - 1)], recv_sem.at[19])
    square = jnp.zeros((BAL, 1), F32)
    for e in range(DP):
        wide = mb[e].astype(F32)
        square += jnp.sum(wide * wide, axis=1, keepdims=True)
    scale = lax.rsqrt(square / D + EPS)
    ri, rj = iota((16, QN * BAL), 0), iota((16, QN * BAL), 1)
    g_bal = (rj % BAL) * T + t
    fits = ((rj // BAL) == (ri // 4)) & ((rj % 4) == (ri % 4))
    back = []
    for o in range(T):
        lo = jnp.concatenate([firsts_i[o * 8:(o + 1) * 8, :QN * BAL]] * 2, axis=0)
        n = jnp.concatenate([counts_i[o * 8:(o + 1) * 8, :QN * BAL]] * 2, axis=0)
        back.append(one_hot(fits & (lo <= g_bal) & (g_bal < lo + n)))
    back = jnp.concatenate(back, axis=0)
    for h in range(per):
        stacked = jnp.concatenate([mb[q * per + h] for q in range(QN)], axis=0)
        for i in range(KE // tile):
            at = h * KE + i * tile
            rts[:, at:at + tile] = dot(back, stacked[:, i * tile:(i + 1) * tile]).astype(BF)
    spread("tensor", T, t, lambda peer: rts.at[aligned(peer, 16), :], rtr.at[aligned(t, 16), :], send_sem.at[21], recv_sem.at[21])
    own_rt = pltpu.make_async_copy(rts.at[aligned(t, 16), :], rtr.at[aligned(t, 16), :], local_sem.at[14])
    own_rt.start()

    own_rp.wait()
    drain(rpr.at[pl.ds(0, DP - 1)], recv_sem.at[20])
    total = rpr[0].astype(F32)
    for e in range(1, DP):
        total += rpr[e].astype(F32)
    total = (total * scale).astype(BF)
    for h in range(T):
        rqs[h] = total[:, h * HEAD:(h + 1) * HEAD]
    spread("tensor", T, t, lambda peer: rqs.at[peer], rq.at[t], send_sem.at[22], recv_sem.at[22])
    own_rq = pltpu.make_async_copy(rqs.at[t], rq.at[t], local_sem.at[15])
    own_rq.start()

    own_ps.wait()
    drain(qr.at[pl.ds(0, NX - 1)], recv_sem.at[18])

    def head_tile(i, carry):
        cols = aligned(i, HEAD)
        total = qr[0, :, cols].astype(F32)
        for e in range(1, NX):
            total += qr[e, :, cols].astype(F32)
        q0s[pl.ds(i, 1)] = total.astype(BF)[None]
        return carry

    lax.fori_loop(0, T, head_tile, 0)
    spread("tensor", T, t, lambda peer: q0s.at[peer], q0r.at[t], send_sem.at[23], recv_sem.at[23])
    own_q0 = pltpu.make_async_copy(q0s.at[t], q0r.at[t], local_sem.at[16])
    own_q0.start()

    own_rt.wait()
    drain(rtr.at[pl.ds(0, (T - 1) * 16), :], recv_sem.at[21])
    g_col = column_of(g_row)
    jl = iota((ROWS, ROUTED), 1)
    hit = ((jl // 16) == (g_col % 16)) & ((jl % 4) == ((g_col // 16) % 4)) & (g_col >= 0)
    for q in range(QN):
        place = one_hot(hit & (((jl // 4) % 4) == q))
        for i in range(CW // tile):
            at = q * CW + i * tile
            moved = dot(place, rtr[:, i * tile:(i + 1) * tile]).astype(BF)
            mix[:, at:at + tile] = jnp.where(g_col >= 0, moved, tok[:, at:at + tile])
    out_mixed = pltpu.make_async_copy(mix, mixed_hbm, local_sem.at[17])
    out_mixed.start()

    own_q0.wait()
    drain(q0r.at[pl.ds(0, T - 1)], recv_sem.at[23])
    own_rq.wait()
    drain(rq.at[pl.ds(0, T - 1)], recv_sem.at[22])
    routed = rq[...].reshape(ROUTED, HEAD)
    g_lane = (jl % 16) * T + jl // 16

    def place_owner(o, carry):
        slots = tabs[pl.ds(o, 1)][0, :1]
        lo = offs[aligned(o, 8), :][:1]
        col = column_of(jnp.where(slots >= 0, slots + lo, -1))
        moved = dot(one_hot(col == g_lane), routed).astype(BF)
        plain = q0r[pl.ds(o, 1)][0]
        qo[aligned(o, ROWS), :] = jnp.where(col >= 0, moved, plain)
        return carry

    lax.fori_loop(0, T, place_owner, 0)
    out_query = pltpu.make_async_copy(qo, query_hbm, local_sem.at[18])
    out_query.start()

    drain(tabs.at[pl.ds(0, T - 1)], send_sem.at[0])
    drain(n0.at[pl.ds(0, DP - 1)], send_sem.at[1])
    drain(a2s.at[pl.ds(0, (T - 1) * 16), :], send_sem.at[2])
    drain(wga.at[pl.ds(0, NY - 1)], send_sem.at[3])
    drain(wqb.at[:, pl.ds(0, 3 * HEAD)], send_sem.at[4])
    drain(wqa.at[:, pl.ds(0, 3 * HEAD)], send_sem.at[5])
    drain(wda.at[pl.ds(0, NY - 1)], send_sem.at[6])
    drain(ns.at[pl.ds(0, DP - 1)], send_sem.at[7])
    drain(rws.at[pl.ds(0, DP - 1)], send_sem.at[8])
    drain(gx.at[pl.ds(0, NZ - 1)], send_sem.at[9])
    drain(wqa.at[:, pl.ds(0, 3 * NY * HEAD)], send_sem.at[10])
    drain(wqb.at[:, pl.ds(0, 3 * NZ * HEAD)], send_sem.at[11])
    drain(gc, send_sem.at[12])
    drain(gs.at[pl.ds(0, NX - 1)], send_sem.at[13])
    drain(hid.at[0, pl.ds(0, NX - 1)], send_sem.at[14])
    drain(hid.at[0], send_sem.at[15])
    drain(dn.at[pl.ds(0, NZ - 1)], send_sem.at[16])
    drain(pc, send_sem.at[17])
    drain(ps.at[pl.ds(0, NX - 1)], send_sem.at[18])
    drain(ms.at[pl.ds(0, DP - 1)], send_sem.at[19])
    drain(rp.at[pl.ds(0, DP - 1)], send_sem.at[20])
    drain(rts.at[pl.ds(0, (T - 1) * 16), :], send_sem.at[21])
    drain(rqs.at[pl.ds(0, T - 1)], send_sem.at[22])
    drain(q0s.at[pl.ds(0, T - 1)], send_sem.at[23])
    out_mixed.wait()
    out_query.wait()


def on_device(tokens, route_order, route_counts, w_router, gain_in, w_gate_up, w_down, gain_next, w_query):
    vmem = pl.BlockSpec(memory_space=pltpu.VMEM)
    anywhere = pl.BlockSpec(memory_space=pl.ANY)
    return pl.pallas_call(
        kernel,
        out_shape=(
            jax.ShapeDtypeStruct((ROWS, D), BF),
            jax.ShapeDtypeStruct((T * ROWS, HEAD), BF),
        ),
        in_specs=[vmem, pl.BlockSpec(memory_space=pltpu.SMEM), vmem, vmem, vmem] + [anywhere] * 4,
        out_specs=(anywhere, anywhere),
        scratch_shapes=[
            pltpu.VMEM((ROWS, D), BF),
            pltpu.VMEM((T, 8, ROWS), I32),
            pltpu.VMEM((ROWS, ROWS), I32),
            pltpu.VMEM((DP, ROWS, KE), BF),
            pltpu.VMEM((DP, ROWS, KE), BF),
            pltpu.VMEM((NY, KE, 2 * UNITS), BF),
            pltpu.VMEM((NY, UNITS, KE), BF),
            pltpu.VMEM((HALF, T * HEAD), BF),
            pltpu.VMEM((HALF, T * HEAD), BF),
            pltpu.VMEM((ROUTED, CW), BF),
            pltpu.VMEM((ROUTED, CW), BF),
            pltpu.VMEM((QN * BAL, CW), F32),
            pltpu.VMEM((DP, BAL, KE), BF),
            pltpu.VMEM((NZ, DP, BAL, KE), BF),
            pltpu.VMEM((DP, BAL, KE + 128), BF),
            pltpu.VMEM((DP, BAL, KE + 128), BF),
            pltpu.VMEM((NC, NX, NZ * LINE // DP, NY * 2 * UNITS), F32),
            pltpu.VMEM((NX, NZ * LINE // DP, NY * 2 * UNITS), F32),
            pltpu.VMEM((NX, NZ * LINE // DP, NY * 2 * UNITS), BF),
            pltpu.VMEM((NX, NZ * LINE // DP, NY * 2 * UNITS), BF),
            pltpu.VMEM((NC, NX, NZ * LINE // DP, NY * UNITS), BF),
            pltpu.VMEM((NZ, LINE, KE), BF),
            pltpu.VMEM((NZ, LINE, KE), BF),
            pltpu.VMEM((NC, NX, ROWS, T * HEAD), BF),
            pltpu.VMEM((NX, ROWS, T * HEAD), BF),
            pltpu.VMEM((NX, ROWS, T * HEAD), BF),
            pltpu.VMEM((NX, ROWS, T * HEAD), BF),
            pltpu.VMEM((T, ROWS, HEAD), BF),
            pltpu.VMEM((T, ROWS, HEAD), BF),
            pltpu.VMEM((DP, BAL, KE), BF),
            pltpu.VMEM((DP, BAL, KE), BF),
            pltpu.VMEM((DP, BAL, T * HEAD), BF),
            pltpu.VMEM((DP, BAL, T * HEAD), BF),
            pltpu.VMEM((T, BAL, HEAD), BF),
            pltpu.VMEM((T, BAL, HEAD), BF),
            pltpu.VMEM((ROUTED, CW), BF),
            pltpu.VMEM((ROUTED, CW), BF),
            pltpu.VMEM((ROWS, D), BF),
            pltpu.VMEM((T * ROWS, HEAD), BF),
            pltpu.SemaphoreType.DMA((19,)),
            pltpu.SemaphoreType.DMA((24,)),
            pltpu.SemaphoreType.DMA((24,)),
        ],
        compiler_params=pltpu.CompilerParams(
            collective_id=0, has_side_effects=True, vmem_limit_bytes=60 * 1024 * 1024
        ),
    )(
        route_order, route_counts, w_router.reshape(1, D), gain_in.reshape(1, D), gain_next.reshape(1, D),
        tokens, w_gate_up, w_down, w_query,
    )


def solution(mesh):
    in_specs = (
        P(("dp", "tensor"), None),
        P(("dp", "tensor"), None),
        P(("dp", "tensor")),
        P(),
        P(),
        P(None, "tensor"),
        P("tensor", None),
        P(),
        P(None, "tensor"),
    )
    out_specs = (P(("dp", "tensor"), None), P("dp", "tensor"))
    return jax.shard_map(
        on_device, mesh=mesh, in_specs=in_specs, out_specs=out_specs, check_vma=False
    )
```

time: 247 us -> 164 us (0.66)
  Pallas kernels: 240 us -> 156 us
    pallas_call x1, Pallas kernels: 240 us -> 156 us  [on_device(): pl.pallas_call(kernel, out_shape=(jax.ShapeDtypeStruct((ROWS, D), BF), ja...]
where the time goes in v2:
time: 164 us; the launch traced here: 163 us
  Pallas kernels  156 us (95%)
  local copies, waits for them, and re-layouts  5.3 us (3%)
    pallas_call x1, Pallas kernels, on_device(): pl.pallas_call(kernel, out_shape=(jax.ShapeDtypeStruct((ROWS, D), BF), ja...  156 us
    unnamed x4, local copies, waits for them, and re-layouts  3.95 us

profile of v2, /device:TPU:1, one launch (start us, length us, event | category | flops | bytes accessed | tf_op | source)
XLA Modules:
  0.0 163.1 jit_solution(1099098600125701835)
XLA Ops:
  1.3 1.4 reshape.13.wr_ref
  2.6 156.5 %shard_map.104 = (bf16[128,8192]{1,0:T(8,128)(2,1)}, bf16[2048,128]{1,0:T(8,128)(2,1)}) custom-call(s32[1,128]{1,0:T(1,128)} %order_ref.1, s32[1]{0:T(128)S(6)} %copy.13.count_ref, bf16[1,8192]{1,0:T(2,128)(2,1)} %reshape.13.wr_ref, f32[1,8192]{1,0:T(1,128)} %bitcast.2, f32[1,8192]{1,0:T(1,128)} %bitcast.3, bf16[128,8192]{1,0:T(8,128)(2,1)} %tok_hbm.1, ...), custom_call_target="tpu_custom_call" | custom-call | tf_op jit(solution)/shard_map/pallas_call | solution.py:467
  159.1 0.0 copy-start
  159.1 3.2 %copy.14 = bf16[128,8192]{1,0:T(8,128)(2,1)} copy(bf16[128,8192]{1,0:T(8,128)(2,1)} %get-tuple-element.4) | data formatting | bytes 4194304
  162.3 0.0 copy-done
  162.3 0.8 copy.15
Async XLA Ops:
  159.1 3.2 %copy-start = (bf16[2048,128]{1,0:T(8,128)(2,1)S(1)}, bf16[2048,128]{1,0:T(8,128)(2,1)}, u32[]{:S(2)}) copy-start(bf16[2048,128]{1,0:T(8,128)(2,1)} %get-tuple-element.5) | copy-start | bytes 1572868

commit v3 on v2

v3 whole, which is shorter than its diff:
```python
import jax
import jax.numpy as jnp
from jax import lax
from jax.experimental import pallas as pl
from jax.experimental.pallas import tpu as pltpu
from jax.sharding import PartitionSpec as P

T = 16
DP = 8
D = 8192
ROWS = 128
HEAD = 128
UNITS = 128
QN = 4
CW = D // QN
KE = D // DP
ROUTED = 256
BAL = ROUTED // T
NZ = 4
NY = 4
NX = 4
NC = 2
LINE = DP * BAL
ZC = NY * HEAD
BLK = NZ * LINE // DP
EPS = 1e-05
MESH = pl.DeviceIdType.MESH
BF = jnp.bfloat16
F32 = jnp.float32
I32 = jnp.int32


def start(source, target, axis, peer, send_sem, recv_sem):
    pltpu.make_async_remote_copy(
        src_ref=source,
        dst_ref=target,
        send_sem=send_sem,
        recv_sem=recv_sem,
        device_id={axis: peer},
        device_id_type=MESH,
    ).start()


def spread(axis, size, me, source, target, send_sem, recv_sem):
    def body(k, carry):
        peer = lax.rem(me + k, size)
        start(source(peer), target, axis, peer, send_sem, recv_sem)
        return carry

    lax.fori_loop(1, size, body, 0)


def drain(view, sem):
    pltpu.make_async_copy(view, view, sem).wait()


def iota(shape, dim):
    return lax.broadcasted_iota(I32, shape, dim)


def dot(a, b):
    return jnp.dot(a, b, preferred_element_type=F32)


def one_hot(mask):
    return jnp.where(mask, 1.0, 0.0).astype(BF)


def aligned(at, size):
    return pl.ds(pl.multiple_of(at * size, size), size)


def column_of(row):
    eye = iota((ROWS, ROWS), 0) == iota((ROWS, ROWS), 1)
    return jnp.sum(jnp.where(eye, row.astype(F32), 0.0), axis=1, keepdims=True).astype(I32)


def kernel(
    order_ref, count_ref, wr_ref, gin_ref, gnx_ref, tok_hbm, wgu_hbm, wd_hbm, wq_hbm,
    mixed_hbm, query_hbm,
    tok, tabs, offs, n0, xr, wga, wda, wqg, a2s, a2r, xb, ns, gx, rws, rwr,
    gp, gc, gs, gr, hid, dn, dr, pq, pc, ps, qr, q0s, q0r, ms, mb, rp, rpr, rqs, rq,
    rts, rtr, mix, qo, spots, spot_m, back,
    local_sem, send_sem, recv_sem, pc_send, pc_recv, qr_send, qr_recv, out_sem,
):
    t = lax.axis_index("tensor")
    d = lax.axis_index("dp")
    z, y = lax.div(t, NY), lax.rem(t, NY)
    x, c = lax.div(d, NC), lax.rem(d, NC)
    sibling = x * NC + 1 - c
    near = (1, 3, 2)
    tile = 512
    per = CW // KE

    def at_y(k):
        return lax.rem(y + k, NY)

    def at_z(k):
        return lax.rem(z + k, NZ)

    def at_x(k):
        return lax.rem(x + k, NX)

    my_k = aligned(d, KE)
    wq_own = wq_hbm.at[my_k, :]
    load_tok = pltpu.make_async_copy(tok_hbm, tok, local_sem.at[0])
    load_tok.start()
    own_wg = pltpu.make_async_copy(wgu_hbm.at[my_k, :], wga.at[y], local_sem.at[1])
    own_wg.start()
    own_wd = pltpu.make_async_copy(wd_hbm.at[:, my_k], wda.at[y], local_sem.at[2])
    own_wd.start()
    own_wq = pltpu.make_async_copy(wq_own, wqg.at[:, aligned(t, HEAD)], local_sem.at[3])
    own_wq.start()

    barrier = pltpu.get_barrier_semaphore()

    def greet_t(k, carry):
        pl.semaphore_signal(barrier, inc=1, device_id={"tensor": lax.rem(t + k, T)}, device_id_type=MESH)
        return carry

    def greet_d(k, carry):
        pl.semaphore_signal(barrier, inc=1, device_id={"dp": lax.rem(d + k, DP)}, device_id_type=MESH)
        return carry

    lax.fori_loop(1, T, greet_t, 0)
    lax.fori_loop(1, DP, greet_d, 0)

    count = count_ref[0]
    slot = iota((8, ROWS), 1)
    values = jnp.where(slot < count, slot + 1, 0).astype(F32).astype(BF)
    pairs = one_hot(iota((ROWS, ROWS), 0) == order_ref[...])
    own = lax.dot_general(values, pairs, (((1,), (1,)), ((), ())), preferred_element_type=F32)
    tabs[pl.ds(t, 1)] = (own.astype(I32) - 1)[None]
    pl.semaphore_wait(barrier, T - 1 + DP - 1)
    spread("tensor", T, t, lambda peer: tabs.at[t], tabs.at[t], send_sem.at[0], recv_sem.at[0])

    start(wq_own, wqg.at[:, aligned(t, HEAD)], "tensor", at_z(2) * NY + y, send_sem.at[1], recv_sem.at[1])
    for k in near:
        start(wq_own, wqg.at[:, aligned(t, HEAD)], "tensor", z * NY + at_y(k), send_sem.at[2], recv_sem.at[2])

    load_tok.wait()
    square = jnp.zeros((ROWS, 1), F32)
    for e in range(DP):
        wide = tok[:, e * KE:(e + 1) * KE].astype(F32)
        square += jnp.sum(wide * wide, axis=1, keepdims=True)
    scale = lax.rsqrt(square / D + EPS)
    for e in range(DP):
        cols = slice(e * KE, (e + 1) * KE)
        n0[e] = (tok[:, cols].astype(F32) * scale * gnx_ref[:, cols]).astype(BF)
    my_n0 = xr.at[c, x]
    for k in (1, 3):
        for i in range(NC):
            peer = at_x(k) * NC + i
            start(n0.at[peer], my_n0, "dp", peer, send_sem.at[3], recv_sem.at[3])
    start(n0.at[sibling], my_n0, "dp", sibling, send_sem.at[3], recv_sem.at[3])
    own_n0 = pltpu.make_async_copy(n0.at[d], my_n0, local_sem.at[4])
    own_n0.start()
    for i in range(NC):
        peer = at_x(2) * NC + i
        start(n0.at[peer], my_n0, "dp", peer, send_sem.at[3], recv_sem.at[3])
    drain(tabs.at[pl.ds(0, T - 1)], recv_sem.at[0])
    marks = one_hot(tabs[...].reshape(T * 8, ROWS) >= 0)
    counts = dot(marks, jnp.ones((ROWS, ROWS), BF))
    sub, lane = iota((ROWS, ROWS), 0), iota((ROWS, ROWS), 1)
    before = one_hot(((lane // 8) < (sub // 8)) & (lane % 8 == 0))
    firsts = dot(before, counts.astype(BF))
    firsts_i, counts_i = firsts.astype(I32), counts.astype(I32)
    offs[...] = firsts_i

    my_first = offs[aligned(t, 8), :][:1]
    my_slots = tabs[pl.ds(t, 1)][0, :1]
    g_row = jnp.where(my_slots >= 0, my_slots + my_first, -1)
    j = iota((ROUTED, ROWS), 0)
    hit = ((j // 16) == (g_row % 16)) & ((j % 4) == ((g_row // 16) % 4)) & (g_row >= 0)
    pick = jnp.concatenate([one_hot(hit & (((j // 4) % 4) == q)) for q in range(QN)], axis=1)
    for i in range(CW // tile):
        stacked = jnp.concatenate([tok[:, q * CW + i * tile:q * CW + (i + 1) * tile] for q in range(QN)], axis=0)
        a2s[:, i * tile:(i + 1) * tile] = dot(pick, stacked).astype(BF)
    spread("tensor", T, t, lambda peer: a2s.at[aligned(peer, 16), :], a2r.at[aligned(t, 16), :], send_sem.at[4], recv_sem.at[4])
    a2r[aligned(t, 16), :] = a2s[aligned(t, 16), :]

    own_wg.wait()
    for k in near:
        start(wga.at[y], wga.at[y], "tensor", z * NY + at_y(k), send_sem.at[5], recv_sem.at[5])

    first_l, last_l = [], []
    for half in range(2):
        group = iota((8, ROWS), 1) // 16
        lo, hi = jnp.zeros((8, ROWS), I32), jnp.zeros((8, ROWS), I32)
        for i in range(8):
            o = half * 8 + i
            f = firsts_i[o * 8:(o + 1) * 8]
            n = counts_i[o * 8:(o + 1) * 8]
            lo = jnp.where(group == i, f, lo)
            hi = jnp.where(group == i, f + n, hi)
        first_l.append(lo)
        last_l.append(hi)
    first_l = jnp.concatenate(first_l, axis=1)[:1]
    last_l = jnp.concatenate(last_l, axis=1)[:1]
    bi, bj = iota((QN * BAL, ROUTED), 0), iota((QN * BAL, ROUTED), 1)
    g_bal = (bi % BAL) * T + t
    compact = one_hot(
        ((bi // BAL) == ((bj // 4) % 4)) & ((bj % 4) == (bi % 4)) & (first_l <= g_bal) & (g_bal < last_l)
    )
    ri, rj = iota((16, QN * BAL), 0), iota((16, QN * BAL), 1)
    g_bal = (rj % BAL) * T + t
    fits = ((rj // BAL) == (ri // 4)) & ((rj % 4) == (ri % 4))
    for o in range(T):
        lo = jnp.concatenate([firsts_i[o * 8:(o + 1) * 8, :QN * BAL]] * 2, axis=0)
        n = jnp.concatenate([counts_i[o * 8:(o + 1) * 8, :QN * BAL]] * 2, axis=0)
        back[o * 16:(o + 1) * 16, :] = one_hot(fits & (lo <= g_bal) & (g_bal < lo + n))
    g_col = column_of(g_row)
    jl = iota((ROWS, ROUTED), 1)
    hit = ((jl // 16) == (g_col % 16)) & ((jl % 4) == ((g_col // 16) % 4)) & (g_col >= 0)
    for q in range(QN):
        spot_m[q] = one_hot(hit & (((jl // 4) % 4) == q))
    g_lane = (jl % 16) * T + jl // 16

    def find_owner(o, carry):
        slots = tabs[pl.ds(o, 1)][0, :1]
        lo = offs[aligned(o, 8), :][:1]
        col = column_of(jnp.where(slots >= 0, slots + lo, -1))
        spots[pl.ds(o, 1)] = one_hot(col == g_lane)[None]
        return carry

    lax.fori_loop(0, T, find_owner, 0)

    drain(a2r.at[pl.ds(0, (T - 1) * 16), :], recv_sem.at[4])
    square, logit = jnp.zeros((BAL, 1), F32), jnp.zeros((BAL, 1), F32)
    xb[...] = dot(compact, a2r[...])
    for q in range(QN):
        rows = xb[q * BAL:(q + 1) * BAL]
        square += jnp.sum(rows * rows, axis=1, keepdims=True)
    scale = lax.rsqrt(square / D + EPS)
    for q in range(QN):
        rows = xb[q * BAL:(q + 1) * BAL] * scale * gin_ref[:, q * CW:(q + 1) * CW]
        for h in range(per):
            ns[q * per + h] = rows[:, h * KE:(h + 1) * KE].astype(BF)
    my_rows = gx.at[z, d]
    spread("dp", DP, d, lambda peer: ns.at[peer], my_rows, send_sem.at[6], recv_sem.at[6])
    gx[pl.ds(z, 1), pl.ds(d, 1)] = ns[pl.ds(d, 1)][None]

    own_wq.wait()
    drain(wqg.at[:, pl.ds(0, 3 * HEAD)], recv_sem.at[2])

    def send_piece(i):
        piece = wqg.at[i * (KE // 4):(i + 1) * (KE // 4), aligned(z, ZC)]
        for k in (1, 3):
            start(piece, piece, "tensor", at_z(k) * NY + y, send_sem.at[7], recv_sem.at[7 if k == 3 else 8])

    send_piece(0)
    for q in range(QN):
        rows = xb[q * BAL:(q + 1) * BAL]
        logit += jnp.sum(rows * wr_ref[:, q * CW:(q + 1) * CW].astype(F32), axis=1, keepdims=True)
        for h in range(per):
            rws[q * per + h, :, :KE] = rows[:, h * KE:(h + 1) * KE].astype(BF)
    weight = 1.0 / (1.0 + jnp.exp(-logit))
    upper = weight.astype(BF)
    lower = (weight - upper.astype(F32)).astype(BF)
    pair = jnp.where(iota((BAL, 128), 1) == 0, upper.astype(F32), lower.astype(F32)).astype(BF)
    for e in range(DP):
        rws[e, :, KE:] = pair
    rwr[pl.ds(d, 1)] = rws[pl.ds(d, 1)]

    drain(gx.at[0, pl.ds(0, DP - 1)], recv_sem.at[6])
    for k in near:
        start(gx.at[z], gx.at[z], "tensor", at_z(k) * NY + y, send_sem.at[9], recv_sem.at[9])
    for i in range(1, 4):
        send_piece(i)
    own_wd.wait()
    for k in near:
        start(wda.at[y], wda.at[y], "tensor", z * NY + at_y(k), send_sem.at[10], recv_sem.at[10])
    drain(wqg.at[:, pl.ds(0, HEAD)], recv_sem.at[1])
    far_head = wqg.at[:, aligned(at_z(2) * NY + y, HEAD)]
    for k in near:
        start(far_head, far_head, "tensor", z * NY + at_y(k), send_sem.at[11], recv_sem.at[11])
    spread("dp", DP, d, lambda peer: rws.at[peer], rwr.at[d], send_sem.at[12], recv_sem.at[12])

    def chunk_product(k):
        rows = xr[...].reshape(DP * ROWS, KE)
        for i in range(2):
            cols = pl.ds(pl.multiple_of(at_z(k) * ZC + i * (ZC // 2), ZC // 2), ZC // 2)
            product = dot(rows, wqg[:, cols]).astype(BF)
            pq[k, :, :, :, i * (ZC // 2):(i + 1) * (ZC // 2)] = product.reshape(NC, NX, ROWS, ZC // 2)
        start(pq.at[k, 1 - c], pc.at[k], "dp", sibling, pc_send.at[k], pc_recv.at[k])

    def chunk_pair(k):
        drain(pc.at[k], pc_recv.at[k])
        for i in range(NX):
            ps[k, i] = (pq[k, c, i].astype(F32) + pc[k, i].astype(F32)).astype(BF)
        for i in near:
            start(ps.at[k, at_x(i)], qr.at[k, i - 1], "dp", at_x(i) * NC + c, qr_send.at[k], qr_recv.at[k])

    def chunk_sum(k):
        drain(qr.at[k], qr_recv.at[k])
        total = ps[k, pl.ds(x, 1)][0].astype(F32)
        for i in range(NX - 1):
            total += qr[k, i].astype(F32)
        total = jnp.where(g_col >= 0, 0.0, total).astype(BF)
        for i in range(NY):
            q0s[k, i] = total[:, i * HEAD:(i + 1) * HEAD]
        for i in range(NY):
            if k > 0 or i > 0:
                start(q0s.at[k, at_y(i)], q0r.at[t], "tensor", at_z(k) * NY + at_y(i), send_sem.at[13], recv_sem.at[13])
        if k == 0:
            q0r[pl.ds(t, 1)] = q0s[0, pl.ds(y, 1)]

    own_n0.wait()
    drain(n0.at[pl.ds(0, DP - 1)], recv_sem.at[3])
    chunk_product(0)
    chunk_pair(0)

    drain(wga.at[pl.ds(0, NY - 1)], recv_sem.at[5])
    drain(gx.at[pl.ds(0, NZ - 1)], recv_sem.at[9])
    rows = gx[...].reshape(NZ * LINE, KE)
    for i in range(NY):
        gp[:, :, :, i * 2 * UNITS:(i + 1) * 2 * UNITS] = dot(rows, wga[i]).reshape(NC, NX, BLK, 2 * UNITS)
    start(gp.at[1 - c], gc, "dp", sibling, send_sem.at[14], recv_sem.at[14])
    drain(gc, recv_sem.at[14])
    for i in range(NX):
        gs[i] = (gp[c, i] + gc[i]).astype(BF)
    for k in near:
        start(gs.at[at_x(k)], gr.at[k - 1], "dp", at_x(k) * NC + c, send_sem.at[15], recv_sem.at[15])
    drain(gr, recv_sem.at[15])
    total = gp[pl.ds(c, 1), pl.ds(x, 1)][0, 0] + gc[pl.ds(x, 1)][0]
    for i in range(NX - 1):
        total += gr[i].astype(F32)
    for i in range(NY):
        gate = total[:, i * 2 * UNITS:i * 2 * UNITS + UNITS]
        up = total[:, i * 2 * UNITS + UNITS:(i + 1) * 2 * UNITS]
        hid[c, pl.ds(x, 1), :, i * UNITS:(i + 1) * UNITS] = (gate / (1.0 + jnp.exp(-gate)) * up).astype(BF)[None]
    for k in near:
        start(hid.at[c, x], hid.at[c, x], "dp", at_x(k) * NC + c, send_sem.at[16], recv_sem.at[16])
    drain(hid.at[0, pl.ds(0, NX - 1)], recv_sem.at[16])
    start(hid.at[c], hid.at[c], "dp", sibling, send_sem.at[17], recv_sem.at[17])

    drain(wda.at[pl.ds(0, NY - 1)], recv_sem.at[10])
    drain(hid.at[0], recv_sem.at[17])
    hidden = hid[...].reshape(NZ * LINE, NY * UNITS)
    down = wda[...].reshape(NY * UNITS, KE)
    for i in range(KE // 256):
        cols = slice(i * 256, (i + 1) * 256)
        dn[:, :, cols] = dot(hidden, down[:, cols]).astype(BF).reshape(NZ, LINE, 256)
    for k in near:
        start(dn.at[at_z(k)], dr.at[k - 1], "tensor", at_z(k) * NY + y, send_sem.at[18], recv_sem.at[18])
    drain(wqg.at[:, pl.ds(0, ZC)], recv_sem.at[7])
    chunk_product(1)
    drain(wqg.at[:, pl.ds(0, ZC)], recv_sem.at[8])
    chunk_product(3)
    chunk_pair(1)
    chunk_sum(0)
    chunk_pair(3)
    drain(rwr.at[pl.ds(0, DP - 1)], recv_sem.at[12])
    drain(dr, recv_sem.at[18])
    branch = dn[pl.ds(z, 1)][0].astype(F32)
    for i in range(NZ - 1):
        branch += dr[i].astype(F32)
    raw = rwr[...].reshape(LINE, KE + 128)
    both = raw[:, KE:].astype(F32)
    weight = both[:, :1] + both[:, 1:2]
    rows = (raw[:, :KE].astype(F32) + weight * branch).astype(BF)
    ms[...] = rows.reshape(DP, BAL, KE)
    spread("dp", DP, d, lambda peer: ms.at[peer], mb.at[d], send_sem.at[19], recv_sem.at[19])
    mb[pl.ds(d, 1)] = ms[pl.ds(d, 1)]
    rows = (rows.astype(F32) * gnx_ref[:, my_k]).astype(BF)
    drain(wqg.at[:, pl.ds(0, 3 * HEAD)], recv_sem.at[11])
    for i in range(T // 2):
        cols = slice(i * 2 * HEAD, (i + 1) * 2 * HEAD)
        rp[:, :, cols] = dot(rows, wqg[:, cols]).astype(BF).reshape(DP, BAL, 2 * HEAD)
    spread("dp", DP, d, lambda peer: rp.at[peer], rpr.at[d], send_sem.at[20], recv_sem.at[20])
    rpr[pl.ds(d, 1)] = rp[pl.ds(d, 1)]
    chunk_product(2)
    chunk_pair(2)
    chunk_sum(1)
    drain(mb.at[pl.ds(0, DP - 1)], recv_sem.at[19])
    square = jnp.zeros((BAL, 1), F32)
    for e in range(DP):
        wide = mb[e].astype(F32)
        square += jnp.sum(wide * wide, axis=1, keepdims=True)
    scale = lax.rsqrt(square / D + EPS)
    for h in range(per):
        stacked = jnp.concatenate([mb[q * per + h] for q in range(QN)], axis=0)
        for i in range(KE // tile):
            at = h * KE + i * tile
            rts[:, at:at + tile] = dot(back[...], stacked[:, i * tile:(i + 1) * tile]).astype(BF)
    spread("tensor", T, t, lambda peer: rts.at[aligned(peer, 16), :], rtr.at[aligned(t, 16), :], send_sem.at[21], recv_sem.at[21])
    rtr[aligned(t, 16), :] = rts[aligned(t, 16), :]

    drain(rpr.at[pl.ds(0, DP - 1)], recv_sem.at[20])
    total = rpr[0].astype(F32)
    for e in range(1, DP):
        total += rpr[e].astype(F32)
    total = (total * scale).astype(BF)
    for h in range(T):
        rqs[h] = total[:, h * HEAD:(h + 1) * HEAD]
    spread("tensor", T, t, lambda peer: rqs.at[peer], rq.at[t], send_sem.at[22], recv_sem.at[23])
    rq[pl.ds(t, 1)] = rqs[pl.ds(t, 1)]
    chunk_sum(3)
    chunk_sum(2)
    drain(rtr.at[pl.ds(0, (T - 1) * 16), :], recv_sem.at[21])
    outs = []
    for q in range(QN):
        for i in range(CW // tile):
            at = q * CW + i * tile
            moved = dot(spot_m[q], rtr[:, i * tile:(i + 1) * tile]).astype(BF)
            mix[:, at:at + tile] = jnp.where(g_col >= 0, moved, tok[:, at:at + tile])
        cols = pl.ds(q * CW, CW)
        copy = pltpu.make_async_copy(mix.at[:, cols], mixed_hbm.at[:, cols], out_sem.at[q])
        copy.start()
        outs.append(copy)

    drain(q0r.at[pl.ds(0, T - 1)], recv_sem.at[13])
    drain(rq.at[pl.ds(0, T - 1)], recv_sem.at[23])
    routed = rq[...].reshape(ROUTED, HEAD)

    def place_owner(o, carry):
        moved = dot(spots[pl.ds(o, 1)][0], routed)
        plain = q0r[pl.ds(o, 1)][0].astype(F32)
        qo[aligned(o, ROWS), :] = (moved + plain).astype(BF)
        return carry

    lax.fori_loop(0, T, place_owner, 0, unroll=4)
    out_query = pltpu.make_async_copy(qo, query_hbm, out_sem.at[QN])
    out_query.start()

    drain(tabs.at[pl.ds(0, T - 1)], send_sem.at[0])
    drain(wqg.at[:, pl.ds(0, HEAD)], send_sem.at[1])
    drain(wqg.at[:, pl.ds(0, 3 * HEAD)], send_sem.at[2])
    drain(n0.at[pl.ds(0, DP - 1)], send_sem.at[3])
    drain(a2s.at[pl.ds(0, (T - 1) * 16), :], send_sem.at[4])
    drain(wga.at[pl.ds(0, NY - 1)], send_sem.at[5])
    drain(ns.at[pl.ds(0, DP - 1)], send_sem.at[6])
    drain(wqg.at[:, pl.ds(0, 2 * ZC)], send_sem.at[7])
    drain(rqs.at[pl.ds(0, T - 1)], send_sem.at[22])
    drain(gx.at[pl.ds(0, NZ - 1)], send_sem.at[9])
    drain(wda.at[pl.ds(0, NY - 1)], send_sem.at[10])
    drain(wqg.at[:, pl.ds(0, 3 * HEAD)], send_sem.at[11])
    drain(rws.at[pl.ds(0, DP - 1)], send_sem.at[12])
    drain(q0r.at[pl.ds(0, T - 1)], send_sem.at[13])
    drain(gc, send_sem.at[14])
    drain(gr, send_sem.at[15])
    drain(hid.at[0, pl.ds(0, NX - 1)], send_sem.at[16])
    drain(hid.at[0], send_sem.at[17])
    drain(dr, send_sem.at[18])
    drain(ms.at[pl.ds(0, DP - 1)], send_sem.at[19])
    drain(rp.at[pl.ds(0, DP - 1)], send_sem.at[20])
    drain(rts.at[pl.ds(0, (T - 1) * 16), :], send_sem.at[21])
    for k in range(NZ):
        drain(pc.at[k], pc_send.at[k])
        drain(qr.at[k], qr_send.at[k])
    for copy in outs:
        copy.wait()
    out_query.wait()


def on_device(tokens, route_order, route_counts, w_router, gain_in, w_gate_up, w_down, gain_next, w_query):
    vmem = pl.BlockSpec(memory_space=pltpu.VMEM)
    anywhere = pl.BlockSpec(memory_space=pl.ANY)
    return pl.pallas_call(
        kernel,
        out_shape=(
            jax.ShapeDtypeStruct((ROWS, D), BF),
            jax.ShapeDtypeStruct((T * ROWS, HEAD), BF),
        ),
        in_specs=[vmem, pl.BlockSpec(memory_space=pltpu.SMEM), vmem, vmem, vmem] + [anywhere] * 4,
        out_specs=(anywhere, anywhere),
        scratch_shapes=[
            pltpu.VMEM((ROWS, D), BF),
            pltpu.VMEM((T, 8, ROWS), I32),
            pltpu.VMEM((ROWS, ROWS), I32),
            pltpu.VMEM((DP, ROWS, KE), BF),
            pltpu.VMEM((NC, NX, ROWS, KE), BF),
            pltpu.VMEM((NY, KE, 2 * UNITS), BF),
            pltpu.VMEM((NY, UNITS, KE), BF),
            pltpu.VMEM((KE, T * HEAD), BF),
            pltpu.VMEM((ROUTED, CW), BF),
            pltpu.VMEM((ROUTED, CW), BF),
            pltpu.VMEM((QN * BAL, CW), F32),
            pltpu.VMEM((DP, BAL, KE), BF),
            pltpu.VMEM((NZ, DP, BAL, KE), BF),
            pltpu.VMEM((DP, BAL, KE + 128), BF),
            pltpu.VMEM((DP, BAL, KE + 128), BF),
            pltpu.VMEM((NC, NX, BLK, NY * 2 * UNITS), F32),
            pltpu.VMEM((NX, BLK, NY * 2 * UNITS), F32),
            pltpu.VMEM((NX, BLK, NY * 2 * UNITS), BF),
            pltpu.VMEM((NX - 1, BLK, NY * 2 * UNITS), BF),
            pltpu.VMEM((NC, NX, BLK, NY * UNITS), BF),
            pltpu.VMEM((NZ, LINE, KE), BF),
            pltpu.VMEM((NZ - 1, LINE, KE), BF),
            pltpu.VMEM((NZ, NC, NX, ROWS, ZC), BF),
            pltpu.VMEM((NZ, NX, ROWS, ZC), BF),
            pltpu.VMEM((NZ, NX, ROWS, ZC), BF),
            pltpu.VMEM((NZ, NX - 1, ROWS, ZC), BF),
            pltpu.VMEM((NZ, NY, ROWS, HEAD), BF),
            pltpu.VMEM((T, ROWS, HEAD), BF),
            pltpu.VMEM((DP, BAL, KE), BF),
            pltpu.VMEM((DP, BAL, KE), BF),
            pltpu.VMEM((DP, BAL, T * HEAD), BF),
            pltpu.VMEM((DP, BAL, T * HEAD), BF),
            pltpu.VMEM((T, BAL, HEAD), BF),
            pltpu.VMEM((T, BAL, HEAD), BF),
            pltpu.VMEM((ROUTED, CW), BF),
            pltpu.VMEM((ROUTED, CW), BF),
            pltpu.VMEM((ROWS, D), BF),
            pltpu.VMEM((T * ROWS, HEAD), BF),
            pltpu.VMEM((T, ROWS, ROUTED), BF),
            pltpu.VMEM((QN, ROWS, ROUTED), BF),
            pltpu.VMEM((ROUTED, QN * BAL), BF),
            pltpu.SemaphoreType.DMA((5,)),
            pltpu.SemaphoreType.DMA((24,)),
            pltpu.SemaphoreType.DMA((24,)),
            pltpu.SemaphoreType.DMA((NZ,)),
            pltpu.SemaphoreType.DMA((NZ,)),
            pltpu.SemaphoreType.DMA((NZ,)),
            pltpu.SemaphoreType.DMA((NZ,)),
            pltpu.SemaphoreType.DMA((QN + 1,)),
        ],
        compiler_params=pltpu.CompilerParams(
            collective_id=0, has_side_effects=True, vmem_limit_bytes=60 * 1024 * 1024
        ),
    )(
        route_order, route_counts, w_router.reshape(1, D), gain_in.reshape(1, D), gain_next.reshape(1, D),
        tokens, w_gate_up, w_down, w_query,
    )


def solution(mesh):
    in_specs = (
        P(("dp", "tensor"), None),
        P(("dp", "tensor"), None),
        P(("dp", "tensor")),
        P(),
        P(),
        P(None, "tensor"),
        P("tensor", None),
        P(),
        P(None, "tensor"),
    )
    out_specs = (P(("dp", "tensor"), None), P("dp", "tensor"))
    return jax.shard_map(
        on_device, mesh=mesh, in_specs=in_specs, out_specs=out_specs, check_vma=False
    )
```

time: 164 us -> 128 us (0.78)
  Pallas kernels: 156 us -> 120 us
    pallas_call x1, Pallas kernels: 156 us -> 120 us  [on_device(): pl.pallas_call(kernel, out_shape=(jax.ShapeDtypeStruct((ROWS, D), BF), ja...]
where the time goes in v3:
time: 128 us; the launch traced here: 126 us
  Pallas kernels  120 us (94%)
  local copies, waits for them, and re-layouts  5.3 us (4%)
  between operations  1.29 us (1%)
    pallas_call x1, Pallas kernels, on_device(): pl.pallas_call(kernel, out_shape=(jax.ShapeDtypeStruct((ROWS, D), BF), ja...  120 us
    unnamed x4, local copies, waits for them, and re-layouts  3.95 us

profile of v3, /device:TPU:1, one launch (start us, length us, event | category | flops | bytes accessed | tf_op | source)
XLA Modules:
  0.0 126.3 jit_solution(2103556967601926370)
XLA Ops:
  1.3 1.4 %reshape.13.wr_ref = bf16[1,8192]{1,0:T(2,128)(2,1)} reshape(bf16[8192]{0:T(1024)(128)(2,1)} %param.12) | data formatting | bytes 32768 | tf_op jit(solution)/shard_map/reshape | solution.py:522
  2.6 119.7 %shard_map.104 = (bf16[128,8192]{1,0:T(8,128)(2,1)}, bf16[2048,128]{1,0:T(8,128)(2,1)}) custom-call(s32[1,128]{1,0:T(1,128)} %order_ref.1, s32[1]{0:T(128)S(6)} %copy.13.count_ref, bf16[1,8192]{1,0:T(2,128)(2,1)} %reshape.13.wr_ref, f32[1,8192]{1,0:T(1,128)} %bitcast.2, f32[1,8192]{1,0:T(1,128)} %bitcast.3, bf16[128,8192]{1,0:T(8,128)(2,1)} %tok_hbm.1, ...), custom_call_target="tpu_custom_call" | custom-call | tf_op jit(solution)/shard_map/pallas_call | solution.py:459
  122.4 0.0 copy-start
  122.4 3.2 %copy.14 = bf16[128,8192]{1,0:T(8,128)(2,1)} copy(bf16[128,8192]{1,0:T(8,128)(2,1)} %get-tuple-element.4) | data formatting | bytes 4194304
  125.5 0.0 copy-done
  125.5 0.8 copy.15
Async XLA Ops:
  122.4 3.2 %copy-start = (bf16[2048,128]{1,0:T(8,128)(2,1)S(1)}, bf16[2048,128]{1,0:T(8,128)(2,1)}, u32[]{:S(2)}) copy-start(bf16[2048,128]{1,0:T(8,128)(2,1)} %get-tuple-element.5) | copy-start | bytes 1572868

commit v4 on v3

v4 whole, which is shorter than its diff:
```python
import jax
import jax.numpy as jnp
from jax import lax
from jax.experimental import pallas as pl
from jax.experimental.pallas import tpu as pltpu
from jax.sharding import PartitionSpec as P

T = 16
DP = 8
D = 8192
ROWS = 128
HEAD = 128
UNITS = 128
QN = 4
CW = D // QN
KE = D // DP
ROUTED = 256
BAL = ROUTED // T
NZ = 4
NY = 4
NX = 4
NC = 2
LINE = DP * BAL
ZC = NY * HEAD
BLK = NZ * LINE // DP
LIMIT = 60
EPS = 1e-05
MESH = pl.DeviceIdType.MESH
BF = jnp.bfloat16
F32 = jnp.float32
I32 = jnp.int32


def start(source, target, axis, peer, send_sem, recv_sem):
    pltpu.make_async_remote_copy(
        src_ref=source,
        dst_ref=target,
        send_sem=send_sem,
        recv_sem=recv_sem,
        device_id={axis: peer},
        device_id_type=MESH,
    ).start()


def spread(axis, size, me, source, target, send_sem, recv_sem):
    def body(k, carry):
        peer = lax.rem(me + k, size)
        start(source(peer), target, axis, peer, send_sem, recv_sem)
        return carry

    lax.fori_loop(1, size, body, 0)


def drain(view, sem):
    pltpu.make_async_copy(view, view, sem).wait()


def iota(shape, dim):
    return lax.broadcasted_iota(I32, shape, dim)


def dot(a, b):
    return jnp.dot(a, b, preferred_element_type=F32)


def one_hot(mask):
    return jnp.where(mask, 1.0, 0.0).astype(BF)


def aligned(at, size):
    return pl.ds(pl.multiple_of(at * size, size), size)


def column_of(row):
    eye = iota((ROWS, ROWS), 0) == iota((ROWS, ROWS), 1)
    return jnp.sum(jnp.where(eye, row.astype(F32), 0.0), axis=1, keepdims=True).astype(I32)


def kernel(
    order_hbm, count_ref, wr_hbm, gin_hbm, gnx_hbm, tok_hbm, wgu_hbm, wd_hbm, wq_hbm,
    mixed_hbm, query_hbm,
    order_ref, wr_ref, gin_ref, gnx_ref, tok, tabs, offs, n0, xr, wga, wda, wqg, a2s, a2r, xb, gx, rws, rwr,
    gp, gc, gs, gr, hid, dn, dr, pq, pc, ps, fr, qr, q0s, q0r, ms, mb, rp, rpc, rps, rpr, rqs, rq,
    rts, rtr, mix, qo, spots, spot_m, back,
    local_sem, send_sem, recv_sem, pc_send, pc_recv, fr_send, fr_recv, qr_send, qr_recv, out_sem,
    dn_send, dn_recv, ms_send, ms_recv, rt_send, rt_recv,
):
    t = lax.axis_index("tensor")
    d = lax.axis_index("dp")
    z, y = lax.div(t, NY), lax.rem(t, NY)
    x, c = lax.div(d, NC), lax.rem(d, NC)
    sibling = x * NC + 1 - c
    near = (1, 3, 2)
    tile = 512
    per = CW // KE

    def at_y(k):
        return lax.rem(y + k, NY)

    def at_z(k):
        return lax.rem(z + k, NZ)

    def at_x(k):
        return lax.rem(x + k, NX)

    def pass_on(part, sem):
        for half, k in ((0, 1), (1, 3)):
            piece = part(at_y(4 - k), half)
            start(piece, piece, "tensor", z * NY + at_y(k), send_sem.at[sem], recv_sem.at[sem])

    my_k = aligned(d, KE)
    wq_own = wq_hbm.at[my_k, :]
    load_order = pltpu.make_async_copy(order_hbm, order_ref, local_sem.at[5])
    load_order.start()
    load_tok = pltpu.make_async_copy(tok_hbm, tok, local_sem.at[0])
    load_tok.start()
    load_gnx = pltpu.make_async_copy(gnx_hbm, gnx_ref, local_sem.at[6])
    load_gnx.start()
    load_gin = pltpu.make_async_copy(gin_hbm, gin_ref, local_sem.at[7])
    load_gin.start()
    load_wr = pltpu.make_async_copy(wr_hbm, wr_ref, local_sem.at[8])
    load_wr.start()
    own_wg = pltpu.make_async_copy(wgu_hbm.at[my_k, :], wga.at[y], local_sem.at[1])
    own_wg.start()
    own_wd = pltpu.make_async_copy(wd_hbm.at[:, my_k], wda.at[y], local_sem.at[2])
    own_wd.start()
    own_wq = pltpu.make_async_copy(wq_own, wqg.at[:, aligned(t, HEAD)], local_sem.at[3])
    own_wq.start()

    barrier = pltpu.get_barrier_semaphore()

    def greet_t(k, carry):
        pl.semaphore_signal(barrier, inc=1, device_id={"tensor": lax.rem(t + k, T)}, device_id_type=MESH)
        return carry

    def greet_d(k, carry):
        pl.semaphore_signal(barrier, inc=1, device_id={"dp": lax.rem(d + k, DP)}, device_id_type=MESH)
        return carry

    lax.fori_loop(1, T, greet_t, 0)
    lax.fori_loop(1, DP, greet_d, 0)

    count = count_ref[0]
    slot = iota((8, ROWS), 1)
    values = jnp.where(slot < count, slot + 1, 0).astype(F32).astype(BF)
    load_order.wait()
    pairs = one_hot(iota((ROWS, ROWS), 0) == order_ref[...])
    own = lax.dot_general(values, pairs, (((1,), (1,)), ((), ())), preferred_element_type=F32)
    tabs[pl.ds(t, 1)] = (own.astype(I32) - 1)[None]

    load_tok.wait()
    load_gnx.wait()
    square = jnp.zeros((ROWS, 1), F32)
    for e in range(DP):
        wide = tok[:, e * KE:(e + 1) * KE].astype(F32)
        square += jnp.sum(wide * wide, axis=1, keepdims=True)
    scale = lax.rsqrt(square / D + EPS)
    for e in range(DP):
        cols = slice(e * KE, (e + 1) * KE)
        n0[e] = (tok[:, cols].astype(F32) * scale * gnx_ref[:, cols]).astype(BF)
    pl.semaphore_wait(barrier, T - 1 + DP - 1)
    spread("tensor", T, t, lambda peer: tabs.at[t], tabs.at[t], send_sem.at[0], recv_sem.at[0])

    start(wq_own, wqg.at[:, aligned(t, HEAD)], "tensor", at_z(2) * NY + y, send_sem.at[1], recv_sem.at[1])
    for k in (1, 3):
        start(wq_own, wqg.at[:, aligned(t, HEAD)], "tensor", z * NY + at_y(k), send_sem.at[2], recv_sem.at[2])

    my_n0 = xr.at[c, x]
    for k in (1, 3):
        for i in range(NC):
            peer = at_x(k) * NC + i
            start(n0.at[peer], my_n0, "dp", peer, send_sem.at[3], recv_sem.at[3])
    start(n0.at[sibling], my_n0, "dp", sibling, send_sem.at[3], recv_sem.at[3])

    def far_n0(i):
        peer = at_x(2) * NC + i
        start(n0.at[peer], my_n0, "dp", peer, send_sem.at[3], recv_sem.at[3])

    own_n0 = pltpu.make_async_copy(n0.at[d], my_n0, local_sem.at[4])
    own_n0.start()
    far_n0(c)
    drain(tabs.at[pl.ds(0, T - 1)], recv_sem.at[0])
    marks = one_hot(tabs[...].reshape(T * 8, ROWS) >= 0)
    counts = dot(marks, jnp.ones((ROWS, ROWS), BF))
    sub, lane = iota((ROWS, ROWS), 0), iota((ROWS, ROWS), 1)
    before = one_hot(((lane // 8) < (sub // 8)) & (lane % 8 == 0))
    firsts = dot(before, counts.astype(BF))
    firsts_i, counts_i = firsts.astype(I32), counts.astype(I32)
    offs[...] = firsts_i

    my_first = offs[aligned(t, 8), :][:1]
    my_slots = tabs[pl.ds(t, 1)][0, :1]
    g_row = jnp.where(my_slots >= 0, my_slots + my_first, -1)
    j = iota((ROUTED, ROWS), 0)
    hit = ((j // 16) == (g_row % 16)) & ((j % 4) == ((g_row // 16) % 4)) & (g_row >= 0)
    pick = jnp.concatenate([one_hot(hit & (((j // 4) % 4) == q)) for q in range(QN)], axis=1)
    for i in range(CW // tile):
        stacked = jnp.concatenate([tok[:, q * CW + i * tile:q * CW + (i + 1) * tile] for q in range(QN)], axis=0)
        a2s[:, i * tile:(i + 1) * tile] = dot(pick, stacked).astype(BF)
    spread("tensor", T, t, lambda peer: a2s.at[aligned(peer, 16), :], a2r.at[aligned(t, 16), :], send_sem.at[4], recv_sem.at[4])
    a2r[aligned(t, 16), :] = a2s[aligned(t, 16), :]

    drain(wqg.at[:, pl.ds(0, 2 * HEAD)], recv_sem.at[2])
    pass_on(lambda at, half: wqg.at[half * (KE // 2):(half + 1) * (KE // 2), aligned(z * NY + at, HEAD)], 7)

    own_wg.wait()
    for k in (1, 3):
        start(wga.at[y], wga.at[y], "tensor", z * NY + at_y(k), send_sem.at[5], recv_sem.at[5])

    first_l, last_l = [], []
    for half in range(2):
        group = iota((8, ROWS), 1) // 16
        lo, hi = jnp.zeros((8, ROWS), I32), jnp.zeros((8, ROWS), I32)
        for i in range(8):
            o = half * 8 + i
            f = firsts_i[o * 8:(o + 1) * 8]
            n = counts_i[o * 8:(o + 1) * 8]
            lo = jnp.where(group == i, f, lo)
            hi = jnp.where(group == i, f + n, hi)
        first_l.append(lo)
        last_l.append(hi)
    first_l = jnp.concatenate(first_l, axis=1)[:1]
    last_l = jnp.concatenate(last_l, axis=1)[:1]
    bi, bj = iota((QN * BAL, ROUTED), 0), iota((QN * BAL, ROUTED), 1)
    g_bal = (bi % BAL) * T + t
    compact = one_hot(
        ((bi // BAL) == ((bj // 4) % 4)) & ((bj % 4) == (bi % 4)) & (first_l <= g_bal) & (g_bal < last_l)
    )
    ri, rj = iota((16, QN * BAL), 0), iota((16, QN * BAL), 1)
    g_bal = (rj % BAL) * T + t
    fits = ((rj // BAL) == (ri // 4)) & ((rj % 4) == (ri % 4))
    for o in range(T):
        lo = jnp.concatenate([firsts_i[o * 8:(o + 1) * 8, :QN * BAL]] * 2, axis=0)
        n = jnp.concatenate([counts_i[o * 8:(o + 1) * 8, :QN * BAL]] * 2, axis=0)
        back[o * 16:(o + 1) * 16, :] = one_hot(fits & (lo <= g_bal) & (g_bal < lo + n))
    g_col = column_of(g_row)
    jl = iota((ROWS, ROUTED), 1)
    hit = ((jl // 16) == (g_col % 16)) & ((jl % 4) == ((g_col // 16) % 4)) & (g_col >= 0)
    for q in range(QN):
        spot_m[q] = one_hot(hit & (((jl // 4) % 4) == q))
    g_lane = (jl % 16) * T + jl // 16

    def find_owner(o, carry):
        slots = tabs[pl.ds(o, 1)][0, :1]
        lo = offs[aligned(o, 8), :][:1]
        col = column_of(jnp.where(slots >= 0, slots + lo, -1))
        spots[pl.ds(o, 1)] = one_hot(col == g_lane)[None]
        return carry

    lax.fori_loop(0, T, find_owner, 0)

    load_gin.wait()
    load_wr.wait()
    drain(a2r.at[pl.ds(0, (T - 1) * 16), :], recv_sem.at[4])
    xb[...] = dot(compact, a2r[...])
    square, logit = jnp.zeros((BAL, 128), F32), jnp.zeros((BAL, 128), F32)
    for q in range(QN):
        rows = xb[q * BAL:(q + 1) * BAL]
        for h in range(per):
            rws[q * per + h, :, :KE] = rows[:, h * KE:(h + 1) * KE].astype(BF)
        for i in range(CW // 128):
            part = rows[:, i * 128:(i + 1) * 128]
            at = q * (CW // 128) + i
            square += part * part
            logit += part * wr_ref[at:at + 1, :].astype(F32)
    scale = lax.rsqrt(jnp.sum(square, axis=1, keepdims=True) / D + EPS)
    weight = 1.0 / (1.0 + jnp.exp(-jnp.sum(logit, axis=1, keepdims=True)))
    terms = []
    for value in (scale, weight):
        for i in range(3):
            terms.append(value.astype(BF).astype(F32))
            value = value - terms[-1]
    at = iota((BAL, 128), 1)
    tail = jnp.zeros((BAL, 128), F32)
    for i in range(6):
        tail = jnp.where(at == i, terms[i], tail)
    for e in range(DP):
        rws[e, :, KE:] = tail.astype(BF)
    spread("dp", DP, d, lambda peer: rws.at[peer], rwr.at[d], send_sem.at[12], recv_sem.at[12])
    rwr[pl.ds(d, 1)] = rws[pl.ds(d, 1)]

    own_wq.wait()
    drain(wqg.at[:, pl.ds(0, HEAD)], recv_sem.at[7])

    def send_piece(i):
        piece = wqg.at[i * (KE // 8):(i + 1) * (KE // 8), aligned(z, ZC)]
        for k in (1, 3):
            start(piece, piece, "tensor", at_z(k) * NY + y, send_sem.at[8], recv_sem.at[8 if k == 3 else 6])

    send_piece(0)

    drain(rwr.at[pl.ds(0, DP - 1)], recv_sem.at[12])
    far_n0(1 - c)
    raw = rwr[...].reshape(LINE, KE + 128)
    both = raw[:, KE:].astype(F32)
    scale = both[:, :1] + both[:, 1:2] + both[:, 2:3]
    line_weight = both[:, 3:4] + both[:, 4:5] + both[:, 5:6]
    normed = (raw[:, :KE].astype(F32) * scale * gin_ref[:, my_k]).astype(BF)
    gx[pl.ds(z, 1)] = normed.reshape(1, DP, BAL, KE)
    for k in near:
        start(gx.at[z], gx.at[z], "tensor", at_z(k) * NY + y, send_sem.at[9], recv_sem.at[9])
    send_piece(1)
    send_piece(2)
    send_piece(3)
    send_piece(4)
    send_piece(5)
    send_piece(6)
    send_piece(7)

    def chunk_product(k):
        rows = xr[...].reshape(DP * ROWS, KE)
        for i in range(2):
            cols = pl.ds(pl.multiple_of(at_z(k) * ZC + i * (ZC // 2), ZC // 2), ZC // 2)
            product = dot(rows, wqg[:, cols]).astype(BF)
            pq[k, :, :, :, i * (ZC // 2):(i + 1) * (ZC // 2)] = product.reshape(NC, NX, ROWS, ZC // 2)
        start(pq.at[k, 1 - c], pc.at[k], "dp", sibling, pc_send.at[k], pc_recv.at[k])

    def chunk_pair(k):
        drain(pc.at[k], pc_recv.at[k])
        for i in range(NX):
            ps[k, i] = (pq[k, c, i].astype(F32) + pc[k, i].astype(F32)).astype(BF)
        for half, i in ((0, 1), (1, 3)):
            part = ps.at[k, at_x(2), half * (ROWS // 2):(half + 1) * (ROWS // 2)]
            start(part, fr.at[k, half], "dp", at_x(i) * NC + c, fr_send.at[k], fr_recv.at[k])

    def chunk_pass(k):
        drain(fr.at[k], fr_recv.at[k])
        for half, i in ((0, 1), (1, 3)):
            rows = slice(half * (ROWS // 2), (half + 1) * (ROWS // 2))
            total = ps[k, pl.ds(at_x(i), 1), rows].astype(F32) + fr[k, half].astype(F32)[None]
            ps[k, pl.ds(at_x(i), 1), rows] = total.astype(BF)
        for half, i in ((0, 1), (1, 3)):
            start(ps.at[k, at_x(i)], qr.at[k, half], "dp", at_x(i) * NC + c, qr_send.at[k], qr_recv.at[k])

    def chunk_sum(k):
        drain(qr.at[k], qr_recv.at[k])
        total = ps[k, pl.ds(x, 1)][0].astype(F32)
        for i in range(2):
            total += qr[k, i].astype(F32)
        total = jnp.where(g_col >= 0, 0.0, total).astype(BF)
        for i in range(NY):
            q0s[k, i] = total[:, i * HEAD:(i + 1) * HEAD]
        for i in range(NY):
            if k > 0 or i > 0:
                start(q0s.at[k, at_y(i)], q0r.at[t], "tensor", at_z(k) * NY + at_y(i), send_sem.at[13], recv_sem.at[13])
        if k == 0:
            q0r[pl.ds(t, 1)] = q0s[0, pl.ds(y, 1)]

    drain(wga.at[pl.ds(0, 2)], recv_sem.at[5])
    pass_on(lambda at, half: wga.at[at, half * (KE // 2):(half + 1) * (KE // 2)], 23)
    own_wd.wait()
    for k in (1, 3):
        start(wda.at[y], wda.at[y], "tensor", z * NY + at_y(k), send_sem.at[10], recv_sem.at[10])
    drain(wqg.at[:, pl.ds(0, HEAD)], recv_sem.at[1])

    def send_far():
        far_head = wqg.at[:, aligned(at_z(2) * NY + y, HEAD)]
        for k in near:
            start(far_head, far_head, "tensor", z * NY + at_y(k), send_sem.at[11], recv_sem.at[11])

    def pass_wda():
        drain(wda.at[pl.ds(0, 2)], recv_sem.at[10])
        pass_on(lambda at, half: wda.at[at, half * (UNITS // 2):(half + 1) * (UNITS // 2)], 25)


    own_n0.wait()
    drain(n0.at[pl.ds(0, DP - 1)], recv_sem.at[3])
    chunk_product(0)
    chunk_pair(0)

    drain(wga.at[0], recv_sem.at[23])
    chunk_pass(0)
    drain(gx.at[pl.ds(0, NZ - 1)], recv_sem.at[9])
    rows = gx[...].reshape(NZ * LINE, KE)
    for i in range(NY):
        gp[i // 2, :, :, :, i % 2 * 2 * UNITS:(i % 2 + 1) * 2 * UNITS] = dot(rows, wga[i]).reshape(NC, NX, BLK, 2 * UNITS)
        if i % 2 == 1:
            start(gp.at[i // 2, 1 - c], gc.at[i // 2], "dp", sibling, send_sem.at[14], recv_sem.at[14])
    drain(gc, recv_sem.at[14])
    for i in range(NX):
        for h in range(2):
            gs[i, :, h * 4 * UNITS:(h + 1) * 4 * UNITS] = (gp[h, c, i] + gc[h, i]).astype(BF)
    for k in near:
        start(gs.at[at_x(k)], gr.at[k - 1], "dp", at_x(k) * NC + c, send_sem.at[15], recv_sem.at[15])
    pass_wda()
    send_far()
    drain(gr, recv_sem.at[15])
    total = jnp.concatenate([gp[h, pl.ds(c, 1), pl.ds(x, 1)][0, 0] + gc[h, pl.ds(x, 1)][0] for h in range(2)], axis=1)
    for i in range(NX - 1):
        total += gr[i].astype(F32)
    for i in range(NY):
        gate = total[:, i * 2 * UNITS:i * 2 * UNITS + UNITS]
        up = total[:, i * 2 * UNITS + UNITS:(i + 1) * 2 * UNITS]
        hid[c, pl.ds(x, 1), :, i * UNITS:(i + 1) * UNITS] = (gate / (1.0 + jnp.exp(-gate)) * up).astype(BF)[None]
    for k in near:
        start(hid.at[c, x], hid.at[c, x], "dp", at_x(k) * NC + c, send_sem.at[16], recv_sem.at[16])
    drain(hid.at[0, pl.ds(0, NX - 1)], recv_sem.at[16])
    start(hid.at[c], hid.at[c], "dp", sibling, send_sem.at[17], recv_sem.at[17])

    drain(wda.at[0], recv_sem.at[25])
    drain(hid.at[0], recv_sem.at[17])
    hidden = hid[...].reshape(NZ * LINE, NY * UNITS)
    down = wda[...].reshape(NY * UNITS, KE)
    for h in range(2):
        for i in range(tile // 256):
            at = h * tile + i * 256
            dn[h, :, :, i * 256:(i + 1) * 256] = dot(hidden, down[:, at:at + 256]).astype(BF).reshape(NZ, LINE, 256)
        for k in near:
            start(dn.at[h, at_z(k)], dr.at[h, k - 1], "tensor", at_z(k) * NY + y, dn_send.at[h], dn_recv.at[h])
    chunk_sum(0)
    drain(wqg.at[:, pl.ds(0, ZC)], recv_sem.at[8])
    chunk_product(1)
    chunk_pair(1)
    drain(wqg.at[:, pl.ds(0, ZC)], recv_sem.at[6])
    chunk_product(3)
    def mix_half(h):
        drain(dr.at[h], dn_recv.at[h])
        branch = dn[h, pl.ds(z, 1)][0].astype(F32)
        for i in range(NZ - 1):
            branch += dr[h, i].astype(F32)
        cols = slice(h * tile, (h + 1) * tile)
        mixed = (raw[:, cols].astype(F32) + line_weight * branch).astype(BF)
        ms[h] = mixed.reshape(DP, BAL, tile)
        spread("dp", DP, d, lambda peer: ms.at[h, peer], mb.at[h, d], ms_send.at[h], ms_recv.at[h])
        mb[h, pl.ds(d, 1)] = ms[h, pl.ds(d, 1)]
        gain = gnx_ref[:, pl.ds(pl.multiple_of(d * KE + h * tile, tile), tile)]
        return (mixed.astype(F32) * gain).astype(BF)

    def return_half(h):
        drain(mb.at[h, pl.ds(0, DP - 1)], ms_recv.at[h])
        for i in range(per):
            stacked = jnp.concatenate([mb[h, q * per + i] for q in range(QN)], axis=0)
            rts[h, :, i * tile:(i + 1) * tile] = dot(back[...], stacked).astype(BF)
        spread("tensor", T, t, lambda peer: rts.at[h, aligned(peer, 16), :], rtr.at[h, aligned(t, 16), :], rt_send.at[h], rt_recv.at[h])
        rtr[h, aligned(t, 16), :] = rts[h, aligned(t, 16), :]

    upper_rows = mix_half(0)
    chunk_pair(3)
    chunk_pass(1)
    drain(wqg.at[:, pl.ds(0, 3 * HEAD)], recv_sem.at[11])
    chunk_product(2)
    return_half(0)
    chunk_pass(3)
    rows = jnp.concatenate([upper_rows, mix_half(1)], axis=1)
    for i in range(T // 2):
        cols = slice(i * 2 * HEAD, (i + 1) * 2 * HEAD)
        product = dot(rows, wqg[:, cols]).astype(BF)
        for e in range(DP):
            rp[e % NC, e // NC, :, cols] = product[e * BAL:(e + 1) * BAL]
    start(rp.at[1 - c], rpc, "dp", sibling, send_sem.at[20], recv_sem.at[20])
    chunk_pair(2)
    drain(rpc, recv_sem.at[20])
    for i in range(NX):
        rps[i] = (rp[c, i].astype(F32) + rpc[i].astype(F32)).astype(BF)
    for k in near:
        start(rps.at[at_x(k)], rpr.at[k - 1], "dp", at_x(k) * NC + c, send_sem.at[6], recv_sem.at[24])
    chunk_sum(1)
    chunk_sum(3)
    return_half(1)
    square = jnp.zeros((BAL, 1), F32)
    for h in range(2):
        for e in range(DP):
            wide = mb[h, e].astype(F32)
            square += jnp.sum(wide * wide, axis=1, keepdims=True)
    scale = lax.rsqrt(square / D + EPS)
    chunk_pass(2)
    drain(rpr, recv_sem.at[24])
    total = rps[pl.ds(x, 1)][0].astype(F32)
    for i in range(NX - 1):
        total += rpr[i].astype(F32)
    total = (total * scale).astype(BF)
    for h in range(T):
        rqs[h] = total[:, h * HEAD:(h + 1) * HEAD]
    spread("tensor", T, t, lambda peer: rqs.at[peer], rq.at[t], send_sem.at[22], recv_sem.at[22])
    rq[pl.ds(t, 1)] = rqs[pl.ds(t, 1)]
    chunk_sum(2)
    for h in range(2):
        drain(rtr.at[h, pl.ds(0, (T - 1) * 16), :], rt_recv.at[h])
    outs = []
    for q in range(QN):
        for i in range(per):
            for h in range(2):
                at = q * CW + i * KE + h * tile
                moved = dot(spot_m[q], rtr[h, :, i * tile:(i + 1) * tile]).astype(BF)
                mix[:, at:at + tile] = jnp.where(g_col >= 0, moved, tok[:, at:at + tile])
        cols = pl.ds(q * CW, CW)
        copy = pltpu.make_async_copy(mix.at[:, cols], mixed_hbm.at[:, cols], out_sem.at[q])
        copy.start()
        outs.append(copy)

    drain(q0r.at[pl.ds(0, T - 1)], recv_sem.at[13])
    drain(rq.at[pl.ds(0, T - 1)], recv_sem.at[22])
    routed = rq[...].reshape(ROUTED, HEAD)

    def place_owner(o, carry):
        moved = dot(spots[pl.ds(o, 1)][0], routed)
        plain = q0r[pl.ds(o, 1)][0].astype(F32)
        qo[aligned(o, ROWS), :] = (moved + plain).astype(BF)
        return carry

    for i in range(NZ):
        for o in range(i * NY, (i + 1) * NY):
            place_owner(o, 0)
        rows = pl.ds(i * NY * ROWS, NY * ROWS)
        copy = pltpu.make_async_copy(qo.at[rows, :], query_hbm.at[rows, :], out_sem.at[QN + i])
        copy.start()
        outs.append(copy)

    drain(tabs.at[pl.ds(0, T - 1)], send_sem.at[0])
    drain(wqg.at[:, pl.ds(0, HEAD)], send_sem.at[1])
    drain(wqg.at[:, pl.ds(0, 2 * HEAD)], send_sem.at[2])
    drain(n0.at[pl.ds(0, DP - 1)], send_sem.at[3])
    drain(a2s.at[pl.ds(0, (T - 1) * 16), :], send_sem.at[4])
    drain(wga.at[pl.ds(0, 2)], send_sem.at[5])
    drain(wqg.at[:, pl.ds(0, HEAD)], send_sem.at[7])
    drain(wqg.at[:, pl.ds(0, 2 * ZC)], send_sem.at[8])
    drain(rqs.at[pl.ds(0, T - 1)], send_sem.at[22])
    drain(wga.at[0], send_sem.at[23])
    drain(gx.at[pl.ds(0, NZ - 1)], send_sem.at[9])
    drain(wda.at[pl.ds(0, 2)], send_sem.at[10])
    drain(wda.at[0], send_sem.at[25])
    drain(wqg.at[:, pl.ds(0, 3 * HEAD)], send_sem.at[11])
    drain(rws.at[pl.ds(0, DP - 1)], send_sem.at[12])
    drain(q0r.at[pl.ds(0, T - 1)], send_sem.at[13])
    drain(gc, send_sem.at[14])
    drain(gr, send_sem.at[15])
    drain(hid.at[0, pl.ds(0, NX - 1)], send_sem.at[16])
    drain(hid.at[0], send_sem.at[17])
    for h in range(2):
        drain(dr.at[h], dn_send.at[h])
        drain(ms.at[h, pl.ds(0, DP - 1)], ms_send.at[h])
        drain(rts.at[h, pl.ds(0, (T - 1) * 16), :], rt_send.at[h])
    drain(rpc, send_sem.at[20])
    drain(rpr, send_sem.at[6])
    for k in range(NZ):
        drain(pc.at[k], pc_send.at[k])
        drain(fr.at[k], fr_send.at[k])
        drain(qr.at[k], qr_send.at[k])
    for copy in outs:
        copy.wait()


def on_device(tokens, route_order, route_counts, w_router, gain_in, w_gate_up, w_down, gain_next, w_query):
    hbm = pl.BlockSpec(memory_space=pltpu.HBM)
    anywhere = pl.BlockSpec(memory_space=pl.ANY)
    return pl.pallas_call(
        kernel,
        out_shape=(
            jax.ShapeDtypeStruct((ROWS, D), BF),
            jax.ShapeDtypeStruct((T * ROWS, HEAD), BF),
        ),
        in_specs=[hbm, pl.BlockSpec(memory_space=pltpu.SMEM)] + [hbm] * 7,
        out_specs=(anywhere, anywhere),
        scratch_shapes=[
            pltpu.VMEM((1, ROWS), I32),
            pltpu.VMEM((D // 128, 128), BF),
            pltpu.VMEM((1, D), F32),
            pltpu.VMEM((1, D), F32),
            pltpu.VMEM((ROWS, D), BF),
            pltpu.VMEM((T, 8, ROWS), I32),
            pltpu.VMEM((ROWS, ROWS), I32),
            pltpu.VMEM((DP, ROWS, KE), BF),
            pltpu.VMEM((NC, NX, ROWS, KE), BF),
            pltpu.VMEM((NY, KE, 2 * UNITS), BF),
            pltpu.VMEM((NY, UNITS, KE), BF),
            pltpu.VMEM((KE, T * HEAD), BF),
            pltpu.VMEM((ROUTED, CW), BF),
            pltpu.VMEM((ROUTED, CW), BF),
            pltpu.VMEM((QN * BAL, CW), F32),
            pltpu.VMEM((NZ, DP, BAL, KE), BF),
            pltpu.VMEM((DP, BAL, KE + 128), BF),
            pltpu.VMEM((DP, BAL, KE + 128), BF),
            pltpu.VMEM((2, NC, NX, BLK, NY * UNITS), F32),
            pltpu.VMEM((2, NX, BLK, NY * UNITS), F32),
            pltpu.VMEM((NX, BLK, NY * 2 * UNITS), BF),
            pltpu.VMEM((NX - 1, BLK, NY * 2 * UNITS), BF),
            pltpu.VMEM((NC, NX, BLK, NY * UNITS), BF),
            pltpu.VMEM((2, NZ, LINE, KE // 2), BF),
            pltpu.VMEM((2, NZ - 1, LINE, KE // 2), BF),
            pltpu.VMEM((NZ, NC, NX, ROWS, ZC), BF),
            pltpu.VMEM((NZ, NX, ROWS, ZC), BF),
            pltpu.VMEM((NZ, NX, ROWS, ZC), BF),
            pltpu.VMEM((NZ, 2, ROWS // 2, ZC), BF),
            pltpu.VMEM((NZ, 2, ROWS, ZC), BF),
            pltpu.VMEM((NZ, NY, ROWS, HEAD), BF),
            pltpu.VMEM((T, ROWS, HEAD), BF),
            pltpu.VMEM((2, DP, BAL, KE // 2), BF),
            pltpu.VMEM((2, DP, BAL, KE // 2), BF),
            pltpu.VMEM((NC, NX, BAL, T * HEAD), BF),
            pltpu.VMEM((NX, BAL, T * HEAD), BF),
            pltpu.VMEM((NX, BAL, T * HEAD), BF),
            pltpu.VMEM((NX - 1, BAL, T * HEAD), BF),
            pltpu.VMEM((T, BAL, HEAD), BF),
            pltpu.VMEM((T, BAL, HEAD), BF),
            pltpu.VMEM((2, ROUTED, CW // 2), BF),
            pltpu.VMEM((2, ROUTED, CW // 2), BF),
            pltpu.VMEM((ROWS, D), BF),
            pltpu.VMEM((T * ROWS, HEAD), BF),
            pltpu.VMEM((T, ROWS, ROUTED), BF),
            pltpu.VMEM((QN, ROWS, ROUTED), BF),
            pltpu.VMEM((ROUTED, QN * BAL), BF),
            pltpu.SemaphoreType.DMA((9,)),
            pltpu.SemaphoreType.DMA((26,)),
            pltpu.SemaphoreType.DMA((26,)),
            pltpu.SemaphoreType.DMA((NZ,)),
            pltpu.SemaphoreType.DMA((NZ,)),
            pltpu.SemaphoreType.DMA((NZ,)),
            pltpu.SemaphoreType.DMA((NZ,)),
            pltpu.SemaphoreType.DMA((NZ,)),
            pltpu.SemaphoreType.DMA((NZ,)),
            pltpu.SemaphoreType.DMA((QN + NZ,)),
            pltpu.SemaphoreType.DMA((2,)),
            pltpu.SemaphoreType.DMA((2,)),
            pltpu.SemaphoreType.DMA((2,)),
            pltpu.SemaphoreType.DMA((2,)),
            pltpu.SemaphoreType.DMA((2,)),
            pltpu.SemaphoreType.DMA((2,)),
        ],
        compiler_params=pltpu.CompilerParams(
            collective_id=0, has_side_effects=True, vmem_limit_bytes=LIMIT * 1024 * 1024
        ),
    )(
        route_order, route_counts, w_router.reshape(D // 128, 128), gain_in.reshape(1, D), gain_next.reshape(1, D),
        tokens, w_gate_up, w_down, w_query,
    )


def solution(mesh):
    in_specs = (
        P(("dp", "tensor"), None),
        P(("dp", "tensor"), None),
        P(("dp", "tensor")),
        P(),
        P(),
        P(None, "tensor"),
        P("tensor", None),
        P(),
        P(None, "tensor"),
    )
    out_specs = (P(("dp", "tensor"), None), P("dp", "tensor"))
    return jax.shard_map(
        on_device, mesh=mesh, in_specs=in_specs, out_specs=out_specs, check_vma=False
    )
```

time: 128 us -> 111 us (0.87)
  Pallas kernels: 120 us -> 105 us
  local copies, waits for them, and re-layouts: 5.3 us -> 3.95 us
    pallas_call x1, Pallas kernels: 120 us -> 105 us  [on_device(): pl.pallas_call(kernel, out_shape=(jax.ShapeDtypeStruct((ROWS, D), BF), ja...]
    reshape x1 -> x0, local copies, waits for them, and re-layouts: 1.35 us -> none  [on_device(): w_router.reshape(1, D)]
where the time goes in v4:
time: 111 us
  Pallas kernels  105 us (95%)
  local copies, waits for them, and re-layouts  3.95 us (4%)
  between operations  1.29 us (1%)
    pallas_call x1, Pallas kernels, on_device(): pl.pallas_call(kernel, out_shape=(jax.ShapeDtypeStruct((ROWS, D), BF), ja...  105 us
    unnamed x4, local copies, waits for them, and re-layouts  3.95 us

profile of v4, /device:TPU:1, one launch (start us, length us, event | category | flops | bytes accessed | tf_op | source)
XLA Modules:
  0.0 110.6 jit_solution(293265141326200366)
XLA Ops:
  1.3 105.3 %shard_map.104 = (bf16[128,8192]{1,0:T(8,128)(2,1)}, bf16[2048,128]{1,0:T(8,128)(2,1)}) custom-call(s32[1,128]{1,0:T(1,128)} %order_hbm.1, s32[1]{0:T(128)S(6)} %copy.13.count_ref, bf16[64,128]{1,0:T(8,128)(2,1)} %bitcast.5, f32[1,8192]{1,0:T(1,128)} %bitcast.3, f32[1,8192]{1,0:T(1,128)} %bitcast.4, bf16[128,8192]{1,0:T(8,128)(2,1)} %tok_hbm.1, ...), custom_call_target="tpu_custom_call" | custom-call | tf_op jit(solution)/shard_map/pallas_call | solution.py:546
  106.6 0.0 copy-start
  106.6 3.2 %copy.14 = bf16[128,8192]{1,0:T(8,128)(2,1)} copy(bf16[128,8192]{1,0:T(8,128)(2,1)} %get-tuple-element.4) | data formatting | bytes 4194304
  109.8 0.0 copy-done
  109.8 0.8 copy.15
Async XLA Ops:
  106.6 3.2 %copy-start = (bf16[2048,128]{1,0:T(8,128)(2,1)S(1)}, bf16[2048,128]{1,0:T(8,128)(2,1)}, u32[]{:S(2)}) copy-start(bf16[2048,128]{1,0:T(8,128)(2,1)} %get-tuple-element.5) | copy-start | bytes 1572868

commit v5 on v4

--- a/solution.py
+++ b/solution.py
@@ -24,6 +24,7 @@
 ZC = NY * HEAD
 BLK = NZ * LINE // DP
 LIMIT = 60
+PARTS = 4
 EPS = 1e-05
 MESH = pl.DeviceIdType.MESH
 BF = jnp.bfloat16
@@ -83,6 +84,7 @@
     gp, gc, gs, gr, hid, dn, dr, pq, pc, ps, fr, qr, q0s, q0r, ms, mb, rp, rpc, rps, rpr, rqs, rq,
     rts, rtr, mix, qo, spots, spot_m, back,
     local_sem, send_sem, recv_sem, pc_send, pc_recv, fr_send, fr_recv, qr_send, qr_recv, out_sem,
+    gc_send, gc_recv, gs_send, gs_recv, hx_send, hx_recv, hc_send, hc_recv,
     dn_send, dn_recv, ms_send, ms_recv, rt_send, rt_recv,
 ):
     t = lax.axis_index("tensor")
@@ -297,15 +299,15 @@
     line_weight = both[:, 3:4] + both[:, 4:5] + both[:, 5:6]
     normed = (raw[:, :KE].astype(F32) * scale * gin_ref[:, my_k]).astype(BF)
     gx[pl.ds(z, 1)] = normed.reshape(1, DP, BAL, KE)
-    for k in near:
+    for k in (1, 3):
         start(gx.at[z], gx.at[z], "tensor", at_z(k) * NY + y, send_sem.at[9], recv_sem.at[9])
     send_piece(1)
-    send_piece(2)
-    send_piece(3)
-    send_piece(4)
-    send_piece(5)
-    send_piece(6)
-    send_piece(7)
+
+    def pass_gx():
+        drain(gx.at[pl.ds(0, 2)], recv_sem.at[9])
+        for half, k in ((0, 1), (1, 3)):
+            piece = gx.at[at_z(4 - k), half * (DP // 2):(half + 1) * (DP // 2)]
+            start(piece, piece, "tensor", at_z(k) * NY + y, send_sem.at[14], recv_sem.at[14])
 
     def chunk_product(k):
         rows = xr[...].reshape(DP * ROWS, KE)
@@ -348,6 +350,13 @@
 
     drain(wga.at[pl.ds(0, 2)], recv_sem.at[5])
     pass_on(lambda at, half: wga.at[at, half * (KE // 2):(half + 1) * (KE // 2)], 23)
+    pass_gx()
+    send_piece(2)
+    send_piece(3)
+    send_piece(4)
+    send_piece(5)
+    send_piece(6)
+    send_piece(7)
     own_wd.wait()
     for k in (1, 3):
         start(wda.at[y], wda.at[y], "tensor", z * NY + at_y(k), send_sem.at[10], recv_sem.at[10])
@@ -370,41 +379,44 @@
 
     drain(wga.at[0], recv_sem.at[23])
     chunk_pass(0)
-    drain(gx.at[pl.ds(0, NZ - 1)], recv_sem.at[9])
+    drain(gx.at[0], recv_sem.at[14])
     rows = gx[...].reshape(NZ * LINE, KE)
     for i in range(NY):
         gp[i // 2, :, :, :, i % 2 * 2 * UNITS:(i % 2 + 1) * 2 * UNITS] = dot(rows, wga[i]).reshape(NC, NX, BLK, 2 * UNITS)
         if i % 2 == 1:
-            start(gp.at[i // 2, 1 - c], gc.at[i // 2], "dp", sibling, send_sem.at[14], recv_sem.at[14])
-    drain(gc, recv_sem.at[14])
-    for i in range(NX):
-        for h in range(2):
-            gs[i, :, h * 4 * UNITS:(h + 1) * 4 * UNITS] = (gp[h, c, i] + gc[h, i]).astype(BF)
-    for k in near:
-        start(gs.at[at_x(k)], gr.at[k - 1], "dp", at_x(k) * NC + c, send_sem.at[15], recv_sem.at[15])
+            start(gp.at[i // 2, 1 - c], gc.at[i // 2], "dp", sibling, gc_send.at[i // 2], gc_recv.at[i // 2])
+    for h in range(2):
+        drain(gc.at[h], gc_recv.at[h])
+        for i in range(NX):
+            gs[h, i] = (gp[h, c, i] + gc[h, i]).astype(BF)
+        for k in near:
+            start(gs.at[h, at_x(k)], gr.at[h, k - 1], "dp", at_x(k) * NC + c, gs_send.at[h], gs_recv.at[h])
     pass_wda()
     send_far()
-    drain(gr, recv_sem.at[15])
-    total = jnp.concatenate([gp[h, pl.ds(c, 1), pl.ds(x, 1)][0, 0] + gc[h, pl.ds(x, 1)][0] for h in range(2)], axis=1)
-    for i in range(NX - 1):
-        total += gr[i].astype(F32)
-    for i in range(NY):
-        gate = total[:, i * 2 * UNITS:i * 2 * UNITS + UNITS]
-        up = total[:, i * 2 * UNITS + UNITS:(i + 1) * 2 * UNITS]
-        hid[c, pl.ds(x, 1), :, i * UNITS:(i + 1) * UNITS] = (gate / (1.0 + jnp.exp(-gate)) * up).astype(BF)[None]
-    for k in near:
-        start(hid.at[c, x], hid.at[c, x], "dp", at_x(k) * NC + c, send_sem.at[16], recv_sem.at[16])
-    drain(hid.at[0, pl.ds(0, NX - 1)], recv_sem.at[16])
-    start(hid.at[c], hid.at[c], "dp", sibling, send_sem.at[17], recv_sem.at[17])
-
+    for h in range(2):
+        drain(gr.at[h], gs_recv.at[h])
+        total = gp[h, pl.ds(c, 1), pl.ds(x, 1)][0, 0] + gc[h, pl.ds(x, 1)][0]
+        for i in range(NX - 1):
+            total += gr[h, i].astype(F32)
+        for i in range(NY // 2):
+            gate = total[:, i * 2 * UNITS:i * 2 * UNITS + UNITS]
+            up = total[:, i * 2 * UNITS + UNITS:(i + 1) * 2 * UNITS]
+            units = (gate / (1.0 + jnp.exp(-gate)) * up).astype(BF)
+            hid[h, pl.ds(c, 1), pl.ds(x, 1), :, i * UNITS:(i + 1) * UNITS] = units[None, None]
+        for k in near:
+            start(hid.at[h, c, x], hid.at[h, c, x], "dp", at_x(k) * NC + c, hx_send.at[h], hx_recv.at[h])
+    for h in range(2):
+        drain(hid.at[h, 0, pl.ds(0, NX - 1)], hx_recv.at[h])
+        start(hid.at[h, c], hid.at[h, c], "dp", sibling, hc_send.at[h], hc_recv.at[h])
     drain(wda.at[0], recv_sem.at[25])
-    drain(hid.at[0], recv_sem.at[17])
-    hidden = hid[...].reshape(NZ * LINE, NY * UNITS)
-    down = wda[...].reshape(NY * UNITS, KE)
+    for h in range(2):
+        drain(hid.at[h, 0], hc_recv.at[h])
+    hidden = [hid[h].reshape(NZ * LINE, NY * UNITS // 2) for h in range(2)]
+    down = wda[...].reshape(2, NY * UNITS // 2, KE)
     for h in range(2):
         for i in range(tile // 256):
             at = h * tile + i * 256
-            dn[h, :, :, i * 256:(i + 1) * 256] = dot(hidden, down[:, at:at + 256]).astype(BF).reshape(NZ, LINE, 256)
+            dn[h, :, :, i * 256:(i + 1) * 256] = (dot(hidden[0], down[0, :, at:at + 256]) + dot(hidden[1], down[1, :, at:at + 256])).astype(BF).reshape(NZ, LINE, 256)
         for k in near:
             start(dn.at[h, at_z(k)], dr.at[h, k - 1], "tensor", at_z(k) * NY + y, dn_send.at[h], dn_recv.at[h])
     chunk_sum(0)
@@ -516,16 +528,18 @@
     drain(wqg.at[:, pl.ds(0, 2 * ZC)], send_sem.at[8])
     drain(rqs.at[pl.ds(0, T - 1)], send_sem.at[22])
     drain(wga.at[0], send_sem.at[23])
-    drain(gx.at[pl.ds(0, NZ - 1)], send_sem.at[9])
+    drain(gx.at[pl.ds(0, 2)], send_sem.at[9])
+    drain(gx.at[0], send_sem.at[14])
     drain(wda.at[pl.ds(0, 2)], send_sem.at[10])
     drain(wda.at[0], send_sem.at[25])
     drain(wqg.at[:, pl.ds(0, 3 * HEAD)], send_sem.at[11])
     drain(rws.at[pl.ds(0, DP - 1)], send_sem.at[12])
     drain(q0r.at[pl.ds(0, T - 1)], send_sem.at[13])
-    drain(gc, send_sem.at[14])
-    drain(gr, send_sem.at[15])
-    drain(hid.at[0, pl.ds(0, NX - 1)], send_sem.at[16])
-    drain(hid.at[0], send_sem.at[17])
+    for h in range(2):
+        drain(gc.at[h], gc_send.at[h])
+        drain(gr.at[h], gs_send.at[h])
+        drain(hid.at[h, 0, pl.ds(0, NX - 1)], hx_send.at[h])
+        drain(hid.at[h, 0], hc_send.at[h])
     for h in range(2):
         drain(dr.at[h], dn_send.at[h])
         drain(ms.at[h, pl.ds(0, DP - 1)], ms_send.at[h])
@@ -540,10 +554,26 @@
         copy.wait()
 
 
+def hand_over(mixed, query, mixed_out, query_out, held_mixed, held_query, in_sem, out_sem):
+    loads, stores = [], []
+    for i in range(PARTS):
+        for j, (source, held, target) in enumerate(((mixed, held_mixed, mixed_out), (query, held_query, query_out))):
+            n = source.shape[0] // PARTS
+            rows = pl.ds(i * n, n)
+            loads.append(pltpu.make_async_copy(source.at[rows, :], held.at[rows, :], in_sem.at[2 * i + j]))
+            stores.append(pltpu.make_async_copy(held.at[rows, :], target.at[rows, :], out_sem.at[2 * i + j]))
+            loads[-1].start()
+    for load, store in zip(loads, stores):
+        load.wait()
+        store.start()
+    for store in stores:
+        store.wait()
+
+
 def on_device(tokens, route_order, route_counts, w_router, gain_in, w_gate_up, w_down, gain_next, w_query):
     hbm = pl.BlockSpec(memory_space=pltpu.HBM)
     anywhere = pl.BlockSpec(memory_space=pl.ANY)
-    return pl.pallas_call(
+    mixed, query = pl.pallas_call(
         kernel,
         out_shape=(
             jax.ShapeDtypeStruct((ROWS, D), BF),
@@ -572,9 +602,9 @@
             pltpu.VMEM((DP, BAL, KE + 128), BF),
             pltpu.VMEM((2, NC, NX, BLK, NY * UNITS), F32),
             pltpu.VMEM((2, NX, BLK, NY * UNITS), F32),
-            pltpu.VMEM((NX, BLK, NY * 2 * UNITS), BF),
-            pltpu.VMEM((NX - 1, BLK, NY * 2 * UNITS), BF),
-            pltpu.VMEM((NC, NX, BLK, NY * UNITS), BF),
+            pltpu.VMEM((2, NX, BLK, NY * UNITS), BF),
+            pltpu.VMEM((2, NX - 1, BLK, NY * UNITS), BF),
+            pltpu.VMEM((2, NC, NX, BLK, NY * UNITS // 2), BF),
             pltpu.VMEM((2, NZ, LINE, KE // 2), BF),
             pltpu.VMEM((2, NZ - 1, LINE, KE // 2), BF),
             pltpu.VMEM((NZ, NC, NX, ROWS, ZC), BF),
@@ -615,6 +645,14 @@
             pltpu.SemaphoreType.DMA((2,)),
             pltpu.SemaphoreType.DMA((2,)),
             pltpu.SemaphoreType.DMA((2,)),
+            pltpu.SemaphoreType.DMA((2,)),
+            pltpu.SemaphoreType.DMA((2,)),
+            pltpu.SemaphoreType.DMA((2,)),
+            pltpu.SemaphoreType.DMA((2,)),
+            pltpu.SemaphoreType.DMA((2,)),
+            pltpu.SemaphoreType.DMA((2,)),
+            pltpu.SemaphoreType.DMA((2,)),
+            pltpu.SemaphoreType.DMA((2,)),
         ],
         compiler_params=pltpu.CompilerParams(
             collective_id=0, has_side_effects=True, vmem_limit_bytes=LIMIT * 1024 * 1024
@@ -623,6 +661,21 @@
         route_order, route_counts, w_router.reshape(D // 128, 128), gain_in.reshape(1, D), gain_next.reshape(1, D),
         tokens, w_gate_up, w_down, w_query,
     )
+    return pl.pallas_call(
+        hand_over,
+        out_shape=(
+            jax.ShapeDtypeStruct((ROWS, D), BF),
+            jax.ShapeDtypeStruct((T * ROWS, HEAD), BF),
+        ),
+        in_specs=[anywhere] * 2,
+        out_specs=(anywhere, anywhere),
+        scratch_shapes=[
+            pltpu.VMEM((ROWS, D), BF),
+            pltpu.VMEM((T * ROWS, HEAD), BF),
+            pltpu.SemaphoreType.DMA((2 * PARTS,)),
+            pltpu.SemaphoreType.DMA((2 * PARTS,)),
+        ],
+    )(mixed, query)
 
 
 def solution(mesh):

time: 111 us -> 108 us (0.973)
  local copies, waits for them, and re-layouts: 3.95 us -> 0 us
    unnamed x4 -> x0, local copies, waits for them, and re-layouts: 3.95 us -> none
    pallas_call x0 -> x1, Pallas kernels: none -> 2.65 us  [on_device(): pl.pallas_call(hand_over, out_shape=(jax.ShapeDtypeStruct((ROWS, D), BF),...]
    pallas_call x1, Pallas kernels: 105 us -> 104 us  [on_device(): pl.pallas_call(kernel, out_shape=(jax.ShapeDtypeStruct((ROWS, D), BF), ja...]
where the time goes in v5:
time: 108 us
  Pallas kernels  106 us (98%)
  between operations  1.29 us (1%)
    pallas_call x1, Pallas kernels, on_device(): pl.pallas_call(kernel, out_shape=(jax.ShapeDtypeStruct((ROWS, D), BF), ja...  104 us
    pallas_call x1, Pallas kernels, on_device(): pl.pallas_call(hand_over, out_shape=(jax.ShapeDtypeStruct((ROWS, D), BF),...  2.65 us

profile of v5, /device:TPU:1, one launch (start us, length us, event | category | flops | bytes accessed | tf_op | source)
XLA Modules:
  0.0 107.6 jit_solution(11950463603004583796)
XLA Ops:
  1.3 103.7 %shard_map.104 = (bf16[128,8192]{1,0:T(8,128)(2,1)}, bf16[2048,128]{1,0:T(8,128)(2,1)}) custom-call(s32[1,128]{1,0:T(1,128)} %order_hbm.1, s32[1]{0:T(128)S(6)} %copy.11.count_ref, bf16[64,128]{1,0:T(8,128)(2,1)} %bitcast.5, f32[1,8192]{1,0:T(1,128)} %bitcast.3, f32[1,8192]{1,0:T(1,128)} %bitcast.4, bf16[128,8192]{1,0:T(8,128)(2,1)} %tok_hbm.1, ...), custom_call_target="tpu_custom_call" | custom-call | tf_op jit(solution)/shard_map/pallas_call | solution.py:576
  105.0 2.7 %shard_map.105 = (bf16[128,8192]{1,0:T(8,128)(2,1)}, bf16[2048,128]{1,0:T(8,128)(2,1)}) custom-call(bf16[128,8192]{1,0:T(8,128)(2,1)} %get-tuple-element.4.mixed, bf16[2048,128]{1,0:T(8,128)(2,1)} %get-tuple-element.5.query), custom_call_target="tpu_custom_call" | custom-call | tf_op jit(solution)/shard_map/pallas_call | solution.py:664

commit v6 on v5

--- a/solution.py
+++ b/solution.py
@@ -83,7 +83,7 @@
     order_ref, wr_ref, gin_ref, gnx_ref, tok, tabs, offs, n0, xr, wga, wda, wqg, a2s, a2r, xb, gx, rws, rwr,
     gp, gc, gs, gr, hid, dn, dr, pq, pc, ps, fr, qr, q0s, q0r, ms, mb, rp, rpc, rps, rpr, rqs, rq,
     rts, rtr, mix, qo, spots, spot_m, back,
-    local_sem, send_sem, recv_sem, pc_send, pc_recv, fr_send, fr_recv, qr_send, qr_recv, out_sem,
+    local_sem, send_sem, recv_sem, pc_send, pc_recv, fr_send, fr_recv, qr_send, qr_recv, q0_recv, out_sem,
     gc_send, gc_recv, gs_send, gs_recv, hx_send, hx_recv, hc_send, hc_recv,
     dn_send, dn_recv, ms_send, ms_recv, rt_send, rt_recv,
 ):
@@ -92,7 +92,7 @@
     z, y = lax.div(t, NY), lax.rem(t, NY)
     x, c = lax.div(d, NC), lax.rem(d, NC)
     sibling = x * NC + 1 - c
-    near = (1, 3, 2)
+    near = (2, 1, 3)
     tile = 512
     per = CW // KE
 
@@ -344,7 +344,7 @@
             q0s[k, i] = total[:, i * HEAD:(i + 1) * HEAD]
         for i in range(NY):
             if k > 0 or i > 0:
-                start(q0s.at[k, at_y(i)], q0r.at[t], "tensor", at_z(k) * NY + at_y(i), send_sem.at[13], recv_sem.at[13])
+                start(q0s.at[k, at_y(i)], q0r.at[t], "tensor", at_z(k) * NY + at_y(i), send_sem.at[13], q0_recv.at[k])
         if k == 0:
             q0r[pl.ds(t, 1)] = q0s[0, pl.ds(y, 1)]
 
@@ -486,38 +486,39 @@
     spread("tensor", T, t, lambda peer: rqs.at[peer], rq.at[t], send_sem.at[22], recv_sem.at[22])
     rq[pl.ds(t, 1)] = rqs[pl.ds(t, 1)]
     chunk_sum(2)
-    for h in range(2):
+    outs = []
+
+    def place_chunk(k):
+        routed = rq[...].reshape(ROUTED, HEAD)
+        if k > 0:
+            drain(q0r.at[pl.ds(0, NY)], q0_recv.at[k])
+        else:
+            drain(q0r.at[pl.ds(0, NY - 1)], q0_recv.at[k])
+        from_z = at_z((NZ - k) % NZ)
+        for i in range(NY):
+            o = from_z * NY + i
+            moved = dot(spots[pl.ds(o, 1)][0], routed)
+            plain = q0r[pl.ds(o, 1)][0].astype(F32)
+            qo[aligned(o, ROWS), :] = (moved + plain).astype(BF)
+        rows = aligned(from_z, NY * ROWS)
+        copy = pltpu.make_async_copy(qo.at[rows, :], query_hbm.at[rows, :], out_sem.at[k])
+        copy.start()
+        outs.append(copy)
+
+    def place_half(h):
         drain(rtr.at[h, pl.ds(0, (T - 1) * 16), :], rt_recv.at[h])
-    outs = []
-    for q in range(QN):
-        for i in range(per):
-            for h in range(2):
+        for q in range(QN):
+            for i in range(per):
                 at = q * CW + i * KE + h * tile
                 moved = dot(spot_m[q], rtr[h, :, i * tile:(i + 1) * tile]).astype(BF)
                 mix[:, at:at + tile] = jnp.where(g_col >= 0, moved, tok[:, at:at + tile])
-        cols = pl.ds(q * CW, CW)
-        copy = pltpu.make_async_copy(mix.at[:, cols], mixed_hbm.at[:, cols], out_sem.at[q])
-        copy.start()
-        outs.append(copy)
-
-    drain(q0r.at[pl.ds(0, T - 1)], recv_sem.at[13])
-    drain(rq.at[pl.ds(0, T - 1)], recv_sem.at[22])
-    routed = rq[...].reshape(ROUTED, HEAD)
-
-    def place_owner(o, carry):
-        moved = dot(spots[pl.ds(o, 1)][0], routed)
-        plain = q0r[pl.ds(o, 1)][0].astype(F32)
-        qo[aligned(o, ROWS), :] = (moved + plain).astype(BF)
-        return carry
-
-    for i in range(NZ):
-        for o in range(i * NY, (i + 1) * NY):
-            place_owner(o, 0)
-        rows = pl.ds(i * NY * ROWS, NY * ROWS)
-        copy = pltpu.make_async_copy(qo.at[rows, :], query_hbm.at[rows, :], out_sem.at[QN + i])
-        copy.start()
-        outs.append(copy)
-
+                cols = pl.ds(at, tile)
+                copy = pltpu.make_async_copy(mix.at[:, cols], mixed_hbm.at[:, cols], out_sem.at[NZ + h * QN * per + q * per + i])
+                copy.start()
+                outs.append(copy)
+
+    place_half(0)
+    place_half(1)
     drain(tabs.at[pl.ds(0, T - 1)], send_sem.at[0])
     drain(wqg.at[:, pl.ds(0, HEAD)], send_sem.at[1])
     drain(wqg.at[:, pl.ds(0, 2 * HEAD)], send_sem.at[2])
@@ -526,7 +527,6 @@
     drain(wga.at[pl.ds(0, 2)], send_sem.at[5])
     drain(wqg.at[:, pl.ds(0, HEAD)], send_sem.at[7])
     drain(wqg.at[:, pl.ds(0, 2 * ZC)], send_sem.at[8])
-    drain(rqs.at[pl.ds(0, T - 1)], send_sem.at[22])
     drain(wga.at[0], send_sem.at[23])
     drain(gx.at[pl.ds(0, 2)], send_sem.at[9])
     drain(gx.at[0], send_sem.at[14])
@@ -534,7 +534,6 @@
     drain(wda.at[0], send_sem.at[25])
     drain(wqg.at[:, pl.ds(0, 3 * HEAD)], send_sem.at[11])
     drain(rws.at[pl.ds(0, DP - 1)], send_sem.at[12])
-    drain(q0r.at[pl.ds(0, T - 1)], send_sem.at[13])
     for h in range(2):
         drain(gc.at[h], gc_send.at[h])
         drain(gr.at[h], gs_send.at[h])
@@ -543,13 +542,21 @@
     for h in range(2):
         drain(dr.at[h], dn_send.at[h])
         drain(ms.at[h, pl.ds(0, DP - 1)], ms_send.at[h])
-        drain(rts.at[h, pl.ds(0, (T - 1) * 16), :], rt_send.at[h])
     drain(rpc, send_sem.at[20])
-    drain(rpr, send_sem.at[6])
     for k in range(NZ):
         drain(pc.at[k], pc_send.at[k])
         drain(fr.at[k], fr_send.at[k])
         drain(qr.at[k], qr_send.at[k])
+    drain(rq.at[pl.ds(0, T - 1)], recv_sem.at[22])
+    place_chunk(0)
+    place_chunk(1)
+    place_chunk(3)
+    place_chunk(2)
+    drain(rqs.at[pl.ds(0, T - 1)], send_sem.at[22])
+    drain(q0r.at[pl.ds(0, T - 1)], send_sem.at[13])
+    drain(rpr, send_sem.at[6])
+    for h in range(2):
+        drain(rts.at[h, pl.ds(0, (T - 1) * 16), :], rt_send.at[h])
     for copy in outs:
         copy.wait()
 
@@ -638,7 +645,8 @@
             pltpu.SemaphoreType.DMA((NZ,)),
             pltpu.SemaphoreType.DMA((NZ,)),
             pltpu.SemaphoreType.DMA((NZ,)),
-            pltpu.SemaphoreType.DMA((QN + NZ,)),
+            pltpu.SemaphoreType.DMA((NZ,)),
+            pltpu.SemaphoreType.DMA((NZ + 2 * QN * (CW // KE),)),
             pltpu.SemaphoreType.DMA((2,)),
             pltpu.SemaphoreType.DMA((2,)),
             pltpu.SemaphoreType.DMA((2,)),

time: 108 us -> 108 us (level)
  no operation moved by 1% of the time
where the time goes in v6:
time: 108 us
  Pallas kernels  106 us (98%)
  between operations  1.29 us (1%)
    pallas_call x1, Pallas kernels, on_device(): pl.pallas_call(kernel, out_shape=(jax.ShapeDtypeStruct((ROWS, D), BF), ja...  104 us
    pallas_call x1, Pallas kernels, on_device(): pl.pallas_call(hand_over, out_shape=(jax.ShapeDtypeStruct((ROWS, D), BF),...  2.65 us

profile of v6, /device:TPU:1, one launch (start us, length us, event | category | flops | bytes accessed | tf_op | source)
XLA Modules:
  0.0 107.8 jit_solution(296500977018070772)
XLA Ops:
  1.3 103.8 %shard_map.104 = (bf16[128,8192]{1,0:T(8,128)(2,1)}, bf16[2048,128]{1,0:T(8,128)(2,1)}) custom-call(s32[1,128]{1,0:T(1,128)} %order_hbm.1, s32[1]{0:T(128)S(6)} %copy.11.count_ref, bf16[64,128]{1,0:T(8,128)(2,1)} %bitcast.5, f32[1,8192]{1,0:T(1,128)} %bitcast.3, f32[1,8192]{1,0:T(1,128)} %bitcast.4, bf16[128,8192]{1,0:T(8,128)(2,1)} %tok_hbm.1, ...), custom_call_target="tpu_custom_call" | custom-call | tf_op jit(solution)/shard_map/pallas_call | solution.py:583
  105.1 2.7 %shard_map.105 = (bf16[128,8192]{1,0:T(8,128)(2,1)}, bf16[2048,128]{1,0:T(8,128)(2,1)}) custom-call(bf16[128,8192]{1,0:T(8,128)(2,1)} %get-tuple-element.4.mixed, bf16[2048,128]{1,0:T(8,128)(2,1)} %get-tuple-element.5.query), custom_call_target="tpu_custom_call" | custom-call | tf_op jit(solution)/shard_map/pallas_call | solution.py:672

commit v7 on v6

--- a/solution.py
+++ b/solution.py
@@ -382,20 +382,20 @@
     drain(gx.at[0], recv_sem.at[14])
     rows = gx[...].reshape(NZ * LINE, KE)
     for i in range(NY):
-        gp[i // 2, :, :, :, i % 2 * 2 * UNITS:(i % 2 + 1) * 2 * UNITS] = dot(rows, wga[i]).reshape(NC, NX, BLK, 2 * UNITS)
+        gp[i // 2, :, :, :, i % 2 * 2 * UNITS:(i % 2 + 1) * 2 * UNITS] = dot(rows, wga[i]).astype(BF).reshape(NC, NX, BLK, 2 * UNITS)
         if i % 2 == 1:
             start(gp.at[i // 2, 1 - c], gc.at[i // 2], "dp", sibling, gc_send.at[i // 2], gc_recv.at[i // 2])
     for h in range(2):
         drain(gc.at[h], gc_recv.at[h])
         for i in range(NX):
-            gs[h, i] = (gp[h, c, i] + gc[h, i]).astype(BF)
+            gs[h, i] = (gp[h, c, i].astype(F32) + gc[h, i].astype(F32)).astype(BF)
         for k in near:
             start(gs.at[h, at_x(k)], gr.at[h, k - 1], "dp", at_x(k) * NC + c, gs_send.at[h], gs_recv.at[h])
     pass_wda()
     send_far()
     for h in range(2):
         drain(gr.at[h], gs_recv.at[h])
-        total = gp[h, pl.ds(c, 1), pl.ds(x, 1)][0, 0] + gc[h, pl.ds(x, 1)][0]
+        total = gp[h, pl.ds(c, 1), pl.ds(x, 1)][0, 0].astype(F32) + gc[h, pl.ds(x, 1)][0].astype(F32)
         for i in range(NX - 1):
             total += gr[h, i].astype(F32)
         for i in range(NY // 2):
@@ -607,8 +607,8 @@
             pltpu.VMEM((NZ, DP, BAL, KE), BF),
             pltpu.VMEM((DP, BAL, KE + 128), BF),
             pltpu.VMEM((DP, BAL, KE + 128), BF),
-            pltpu.VMEM((2, NC, NX, BLK, NY * UNITS), F32),
-            pltpu.VMEM((2, NX, BLK, NY * UNITS), F32),
+            pltpu.VMEM((2, NC, NX, BLK, NY * UNITS), BF),
+            pltpu.VMEM((2, NX, BLK, NY * UNITS), BF),
             pltpu.VMEM((2, NX, BLK, NY * UNITS), BF),
             pltpu.VMEM((2, NX - 1, BLK, NY * UNITS), BF),
             pltpu.VMEM((2, NC, NX, BLK, NY * UNITS // 2), BF),

time: 108 us -> 108 us (level)
  no operation moved by 1% of the time
where the time goes in v7:
time: 108 us
  Pallas kernels  107 us (99%)
  between operations  1.29 us (1%)
    pallas_call x1, Pallas kernels, on_device(): pl.pallas_call(kernel, out_shape=(jax.ShapeDtypeStruct((ROWS, D), BF), ja...  104 us
    pallas_call x1, Pallas kernels, on_device(): pl.pallas_call(hand_over, out_shape=(jax.ShapeDtypeStruct((ROWS, D), BF),...  2.65 us

profile of v7, /device:TPU:1, one launch (start us, length us, event | category | flops | bytes accessed | tf_op | source)
XLA Modules:
  0.0 107.9 jit_solution(15238421428731557711)
XLA Ops:
  1.3 103.9 %shard_map.104 = (bf16[128,8192]{1,0:T(8,128)(2,1)}, bf16[2048,128]{1,0:T(8,128)(2,1)}) custom-call(s32[1,128]{1,0:T(1,128)} %order_hbm.1, s32[1]{0:T(128)S(6)} %copy.11.count_ref, bf16[64,128]{1,0:T(8,128)(2,1)} %bitcast.5, f32[1,8192]{1,0:T(1,128)} %bitcast.3, f32[1,8192]{1,0:T(1,128)} %bitcast.4, bf16[128,8192]{1,0:T(8,128)(2,1)} %tok_hbm.1, ...), custom_call_target="tpu_custom_call" | custom-call | tf_op jit(solution)/shard_map/pallas_call | solution.py:583
  105.2 2.7 %shard_map.105 = (bf16[128,8192]{1,0:T(8,128)(2,1)}, bf16[2048,128]{1,0:T(8,128)(2,1)}) custom-call(bf16[128,8192]{1,0:T(8,128)(2,1)} %get-tuple-element.4.mixed, bf16[2048,128]{1,0:T(8,128)(2,1)} %get-tuple-element.5.query), custom_call_target="tpu_custom_call" | custom-call | tf_op jit(solution)/shard_map/pallas_call | solution.py:672
